TPU v7x, 32 devices: a whole 2x2x4 slice. The times are simulated.
32 devices in a mesh: row: 8 (over z, y), col: 4 (over x, core).
Axes of the slice: x: 2, y: 2, z: 4, core: 2. Of those that a mesh axis runs over, the one named last changes fastest.
Arguments:
- covariance: float32 [2048, 2048], P('row', 'col')
- courants: float32 [2, 2, 16, 128], replicated, may hold values from -0.9 to 0.9
- process_noise_spread: float32 [16, 128], P('row'), may hold values from 0.1 to 1
- sensor_targets: int32 [128], replicated, may hold values from 0 to 2047, as said below
- noise_variance: float32 [128], replicated, may hold values from 0.2 to 1
Outputs:
- posterior_spread: float32 [2048, 2048], P('row', 'col')
Inputs may be any that keep to these rules, and one draw needn't show every extreme that they name: `sensor_targets`: sorted ascending, all distinct; exactly 16 of them lie in each band of 256 consecutive state indices that starts at a multiple of 256.
All inputs are finite; a program needn't handle non-finite values.
Results may differ from a plain program's by a relative error of at most 0.0003.
Values sent between devices are 32-bit elements; how exact they have to be, the bound alone decides.
A program may use at most 64 MiB of HBM per device.

v0:
```python
import jax
import jax.numpy as jnp
from jax import lax
from jax.sharding import PartitionSpec as P

NC = 128
CYCLES = 2


finest_accuracy = lax.Precision.HIGHEST


def padded_2(array, sides, width):
    for axis, dim in sides:
        size, length = (lax.axis_size(axis), array.shape[dim])
        up = [(i, (i + 1) % size) for i in range(size)]
        down = [(j, i) for i, j in up]
        last = lax.slice_in_dim(array, length - width, length, axis=dim)
        initial = lax.slice_in_dim(array, 0, width, axis=dim)
        before = lax.ppermute(last, axis, up)
        after = lax.ppermute(initial, axis, down)
        array = jnp.concatenate([before, array, after], axis=dim)
    return array


def stencil_weights(courant):
    return (
        courant * (1.0 + courant) * 0.5,
        1.0 - courant * courant,
        courant * (courant - 1.0) * 0.5,
    )


def sweep_local(joint_spread_array, courant, which_axis):
    weight_behind, weight_centre, weight_ahead = stencil_weights(courant)
    return (
        weight_behind * jnp.roll(joint_spread_array, 1, which_axis)
        + weight_centre * joint_spread_array
        + weight_ahead * jnp.roll(joint_spread_array, -1, which_axis)
    )


def sweep_padded(padded, courant, which_axis, keep_rows):
    weight_behind, weight_centre, weight_ahead = stencil_weights(courant)
    lower_rows = lax.slice_in_dim(padded, 0, keep_rows, axis=which_axis)
    middle = lax.slice_in_dim(padded, 1, keep_rows + 1, axis=which_axis)
    upper_rows = lax.slice_in_dim(padded, 2, keep_rows + 2, axis=which_axis)
    return weight_behind * lower_rows + weight_centre * middle + weight_ahead * upper_rows


def wind_rows(courants, cycle_index, component, offset, length):
    surface = courants[cycle_index, component]
    extent_rows = surface.shape[0]
    doubled = jnp.concatenate([surface, surface], axis=0)
    return lax.dynamic_slice_in_dim(doubled, jnp.mod(offset, extent_rows), length, 0)


def per_device(covariance, courants, process_noise_spread, sensor_targets, noise_variance):
    row_index = lax.axis_index("row")
    column_index = lax.axis_index("col")
    row_total = lax.axis_size("row")
    column_total = lax.axis_size("col")
    horizontal_tile_piece, vertical_tile_piece = covariance.shape
    band_rows = horizontal_tile_piece // NC
    band_columns = vertical_tile_piece // NC
    row_first = row_index * band_rows
    column_first = column_index * band_columns
    joint_spread_array = covariance
    for cycle_index in range(CYCLES):
        joint_spread_array = joint_spread_array.reshape(band_rows, NC, vertical_tile_piece)
        eastward = wind_rows(courants, cycle_index, 0, row_first, band_rows)[:, :, None]
        joint_spread_array = sweep_local(joint_spread_array, eastward, 1)
        padded = padded_2(joint_spread_array, (("row", 0),), 1)
        northward = wind_rows(courants, cycle_index, 1, row_first, band_rows)[:, :, None]
        joint_spread_array = sweep_padded(padded, northward, 0, band_rows)
        joint_spread_array = joint_spread_array.reshape(horizontal_tile_piece, band_columns, NC)
        eastward = wind_rows(courants, cycle_index, 0, column_first, band_columns)[None]
        joint_spread_array = sweep_local(joint_spread_array, eastward, 2)
        padded = padded_2(joint_spread_array, (("col", 1),), 1)
        northward = wind_rows(courants, cycle_index, 1, column_first, band_columns)[None]
        joint_spread_array = sweep_padded(padded, northward, 1, band_columns)
    predicted_spread = joint_spread_array.reshape(horizontal_tile_piece, vertical_tile_piece)
    row_ids = row_index * horizontal_tile_piece + jnp.arange(horizontal_tile_piece, dtype=jnp.int32)
    column_ids = column_index * vertical_tile_piece + jnp.arange(
        vertical_tile_piece, dtype=jnp.int32
    )
    predicted_spread = predicted_spread + jnp.where(
        row_ids[:, None] == column_ids[None, :],
        process_noise_spread.reshape(horizontal_tile_piece, 1),
        0.0,
    )
    station_total = sensor_targets.shape[0]
    row_share = station_total // row_total
    column_share = station_total // column_total
    sensor_horizontal_indices = (
        lax.dynamic_slice_in_dim(sensor_targets, row_index * row_share, row_share)
        - row_index * horizontal_tile_piece
    )
    sensor_vertical_indices = (
        lax.dynamic_slice_in_dim(sensor_targets, column_index * column_share, column_share)
        - column_index * vertical_tile_piece
    )
    sensor_horizontal_tile = jnp.take(predicted_spread, sensor_horizontal_indices, axis=0)
    tile_update_weighting = jnp.take(predicted_spread, sensor_vertical_indices, axis=1)
    innovation_block = jnp.take(sensor_horizontal_tile, sensor_vertical_indices, axis=1)
    strip = lax.all_gather(innovation_block, "col", axis=1, tiled=True)
    innovation = lax.all_gather(strip, "row", axis=0, tiled=True)
    innovation = innovation + jnp.diag(noise_variance)
    factor = jnp.linalg.cholesky(innovation)
    inverse = jax.scipy.linalg.solve_triangular(
        factor, jnp.eye(station_total, dtype=jnp.float32), lower=True
    )
    columns = inverse
    lower_triangle_target = jnp.dot(
        columns,
        lax.all_gather(sensor_horizontal_tile, "row", axis=0, tiled=True),
        precision=finest_accuracy,
    )
    columns = inverse
    lower_triangle_source = lax.dot_general(
        columns,
        lax.all_gather(tile_update_weighting, "col", axis=1, tiled=True),
        (((1,), (1,)), ((), ())),
        precision=finest_accuracy,
    )
    posterior_spread = predicted_spread - lax.dot_general(
        lower_triangle_source,
        lower_triangle_target,
        (((0,), (0,)), ((), ())),
        precision=finest_accuracy,
    )
    return posterior_spread


def solution(mesh):
    in_specs = (P("row", "col"), P(), P("row", None), P(), P())
    out_specs = P("row", "col")
    return jax.shard_map(
        per_device, mesh=mesh, in_specs=in_specs, out_specs=out_specs, check_vma=False
    )
```

profile of v0, /device:TPU:0, one launch (start us, length us, event | category | flops | bytes accessed | tf_op | source)
XLA Modules:
  0.0 149.9 jit_solution(6708047676042164893)
XLA Ops:
  0.0 1.4 fusion.70
  1.5 0.2 fusion.17
  1.8 3.0 %collective-permute-start = (f32[1,128,512]{2,1,0:T(8,128)S(1)}, f32[1,128,512]{2,1,0:T(8,128)S(1)}, u32[]{:S(2)}, u32[]{:S(2)}) collective-permute-start(f32[1,128,512]{2,1,0:T(8,128)S(1)} %get-tuple-element.43), channel_id=1, source_target_pairs={{0,4},{4,8},{8,12},{12,16},{16,20},{20,24},{24,28},{28,0},{1,5},{5... | collective-permute-start | bytes 786440 | tf_op jit(solution)/shard_map/ppermute | solution.py:20
  4.8 3.1 %collective-permute-start.1 = (f32[1,128,512]{2,1,0:T(8,128)S(1)}, f32[1,128,512]{2,1,0:T(8,128)S(1)}, u32[]{:S(2)}, u32[]{:S(2)}) collective-permute-start(f32[1,128,512]{2,1,0:T(8,128)S(1)} %get-tuple-element.44), channel_id=1, source_target_pairs={{4,0},{8,4},{12,8},{16,12},{20,16},{24,20},{28,24},{0,28},{5,1},{9... | collective-permute-start | bytes 786440 | tf_op jit(solution)/shard_map/ppermute | solution.py:21
  8.1 7.8 %collective-permute-done = f32[1,128,512]{2,1,0:T(8,128)S(1)} collective-permute-done((f32[1,128,512]{2,1,0:T(8,128)S(1)}, f32[1,128,512]{2,1,0:T(8,128)S(1)}, u32[]{:S(2)}, u32[]{:S(2)}) %collective-permute-start) | collective-permute-done | bytes 262176 | tf_op jit(solution)/shard_map/ppermute | solution.py:20
  16.0 2.2 %collective-permute-done.1 = f32[1,128,512]{2,1,0:T(8,128)S(1)} collective-permute-done((f32[1,128,512]{2,1,0:T(8,128)S(1)}, f32[1,128,512]{2,1,0:T(8,128)S(1)}, u32[]{:S(2)}, u32[]{:S(2)}) %collective-permute-start.1) | collective-permute-done | bytes 262176 | tf_op jit(solution)/shard_map/ppermute | solution.py:21
  18.2 0.2 fusion.13
  18.3 0.2 reshape.135
  18.5 0.3 fusion.67
  18.9 0.3 fusion.68
  19.2 0.7 fusion.19
  19.9 0.2 fusion.66
  20.2 1.7 %collective-permute-start.3 = (f32[256,1,128]{2,1,0:T(1,128)S(1)}, f32[256,1,128]{2,1,0:T(1,128)S(1)}, u32[]{:S(2)}, u32[]{:S(2)}) collective-permute-start(f32[256,1,128]{2,1,0:T(1,128)S(1)} %get-tuple-element.38), channel_id=1, source_target_pairs={{1,0},{2,1},{3,2},{0,3},{5,4},{6,5},{7,6},{4,7},{9,8},{10,9},{11,1... | collective-permute-start | bytes 393224 | tf_op jit(solution)/shard_map/ppermute | solution.py:21
  22.0 2.6 %collective-permute-done.2 = f32[256,1,128]{2,1,0:T(1,128)S(1)} collective-permute-done((f32[256,1,128]{2,1,0:T(1,128)S(1)}, f32[256,1,128]{2,1,0:T(1,128)S(1)}, u32[]{:S(2)}, u32[]{:S(2)}) %collective-permute-start.2) | collective-permute-done | bytes 131104 | tf_op jit(solution)/shard_map/ppermute | solution.py:20
  24.6 0.4 collective-permute-done.3
  25.0 0.6 fusion.9
  25.6 0.2 reshape.136
  25.9 0.2 fusion.21
  26.2 0.3 collective-permute-start.4
  26.5 4.4 %collective-permute-start.5 = (f32[1,128,512]{2,1,0:T(8,128)S(1)}, f32[1,128,512]{2,1,0:T(8,128)S(1)}, u32[]{:S(2)}, u32[]{:S(2)}) collective-permute-start(f32[1,128,512]{2,1,0:T(8,128)S(1)} %get-tuple-element.32), channel_id=1, source_target_pairs={{4,0},{8,4},{12,8},{16,12},{20,16},{24,20},{28,24},{0,28},{5,1},{9... | collective-permute-start | bytes 786440 | tf_op jit(solution)/shard_map/ppermute | solution.py:21
  31.0 7.6 %collective-permute-done.4 = f32[1,128,512]{2,1,0:T(8,128)S(1)} collective-permute-done((f32[1,128,512]{2,1,0:T(8,128)S(1)}, f32[1,128,512]{2,1,0:T(8,128)S(1)}, u32[]{:S(2)}, u32[]{:S(2)}) %collective-permute-start.4) | collective-permute-done | bytes 262176 | tf_op jit(solution)/shard_map/ppermute | solution.py:20
  38.6 2.9 %collective-permute-done.5 = f32[1,128,512]{2,1,0:T(8,128)S(1)} collective-permute-done((f32[1,128,512]{2,1,0:T(8,128)S(1)}, f32[1,128,512]{2,1,0:T(8,128)S(1)}, u32[]{:S(2)}, u32[]{:S(2)}) %collective-permute-start.5) | collective-permute-done | bytes 262176 | tf_op jit(solution)/shard_map/ppermute | solution.py:21
  41.6 0.2 reshape.137
  41.8 0.3 fusion.61
  42.2 0.3 fusion.62
  42.5 0.7 fusion.23
  43.2 0.2 fusion.60
  43.6 1.6 %collective-permute-start.7 = (f32[256,1,128]{2,1,0:T(1,128)S(1)}, f32[256,1,128]{2,1,0:T(1,128)S(1)}, u32[]{:S(2)}, u32[]{:S(2)}) collective-permute-start(f32[256,1,128]{2,1,0:T(1,128)S(1)} %get-tuple-element.26), channel_id=1, source_target_pairs={{1,0},{2,1},{3,2},{0,3},{5,4},{6,5},{7,6},{4,7},{9,8},{10,9},{11,1... | collective-permute-start | bytes 393224 | tf_op jit(solution)/shard_map/ppermute | solution.py:21
  45.3 2.6 %collective-permute-done.6 = f32[256,1,128]{2,1,0:T(1,128)S(1)} collective-permute-done((f32[256,1,128]{2,1,0:T(1,128)S(1)}, f32[256,1,128]{2,1,0:T(1,128)S(1)}, u32[]{:S(2)}, u32[]{:S(2)}) %collective-permute-start.6) | collective-permute-done | bytes 131104 | tf_op jit(solution)/shard_map/ppermute | solution.py:20
  47.9 0.5 collective-permute-done.7
  48.3 0.6 fusion.1
  48.9 0.7 copy-done.4
  49.8 0.6 gather_fusion
  50.5 30.7 %all_gather.15 = f32[128,512]{1,0:T(8,128)S(1)} all-gather(f32[16,512]{1,0:T(8,128)S(1)} %broadcast_select_fusion), channel_id=1, replica_groups=mesh['row'=8,'col'=4] {'row'}, dimensions={0}, use_global_device_ids=true | all-gather | bytes 294912 | tf_op jit(solution)/shard_map/all_gather | solution.py:116
  81.3 0.2 copy.14
  81.5 0.6 gather_fusion.1
  82.2 5.2 %all-gather = f32[4,32,16]{1,2,0:T(8,128)S(1)} all-gather(f32[1,32,16]{1,2,0:T(8,128)S(1)} %copy.11), channel_id=1, replica_groups=mesh['row'=8,'col'=4] {'col'}, dimensions={0}, use_global_device_ids=true | all-gather | bytes 10240 | tf_op jit(solution)/shard_map/all_gather | solution.py:106
  87.5 30.8 %all_gather.13 = f32[128,128]{1,0:T(8,128)S(1)} all-gather(f32[16,128]{1,0:T(8,128)S(1)} %bitcast.39), channel_id=1, replica_groups=mesh['row'=8,'col'=4] {'row'}, dimensions={0}, use_global_device_ids=true | all-gather | bytes 73728 | tf_op jit(solution)/shard_map/all_gather | solution.py:107
  118.6 11.7 %cholesky.17 = f32[128,128]{1,0:T(8,128)S(1)} custom-call(f32[128,128]{1,0:T(8,128)S(1)} %fusion.27), custom_call_target="Cholesky" | custom-call | tf_op jit(solution)/shard_map/jit(cholesky)/cholesky | solution.py:109
  130.3 0.6 compare_reduce_fusion
  131.0 0.7 fusion.24
  131.6 9.8 %custom-call.7 = f32[1,128,128]{1,2,0:T(8,128)S(1)} custom-call(f32[1,128,128]{2,1,0:T(8,128)S(1)} %fusion.24), custom_call_target="InvertDiagBlocksLowerTriangular" | custom-call | tf_op jit(solution)/shard_map/jit(_solve_triangular)/triangular_solve | solution.py:110
  141.5 0.2 fusion.25
  141.7 0.6 gather_fusion.2
  142.4 5.4 %all_gather.14 = f32[256,128]{0,1:T(8,128)S(1)} all-gather(f32[256,32]{0,1:T(8,128)S(1)} %select_bitcast_fusion), channel_id=1, replica_groups=mesh['row'=8,'col'=4] {'col'}, dimensions={1}, use_global_device_ids=true | all-gather | bytes 163840 | tf_op jit(solution)/shard_map/all_gather | solution.py:122
  147.8 0.4 fusion.73
  148.2 0.3 fusion.72
  148.4 1.4 convolution_subtract_fusion
  (52 shorter events, 1.9 us)
Async XLA Ops:
  0.0 1.4 copy-start
  0.0 1.5 copy-start.1
  1.8 14.2 %collective-permute-start = (f32[1,128,512]{2,1,0:T(8,128)S(1)}, f32[1,128,512]{2,1,0:T(8,128)S(1)}, u32[]{:S(2)}, u32[]{:S(2)}) collective-permute-start(f32[1,128,512]{2,1,0:T(8,128)S(1)} %get-tuple-element.43), channel_id=1, source_target_pairs={{0,4},{4,8},{8,12},{12,16},{16,20},{20,24},{24,28},{28,0},{1,5},{5... | collective-permute-start | bytes 786440 | tf_op jit(solution)/shard_map/ppermute | solution.py:20
  4.8 13.4 %collective-permute-start.1 = (f32[1,128,512]{2,1,0:T(8,128)S(1)}, f32[1,128,512]{2,1,0:T(8,128)S(1)}, u32[]{:S(2)}, u32[]{:S(2)}) collective-permute-start(f32[1,128,512]{2,1,0:T(8,128)S(1)} %get-tuple-element.44), channel_id=1, source_target_pairs={{4,0},{8,4},{12,8},{16,12},{20,16},{24,20},{28,24},{0,28},{5,1},{9... | collective-permute-start | bytes 786440 | tf_op jit(solution)/shard_map/ppermute | solution.py:21
  20.1 1.8 %copy-start.3 = (s32[128]{0:T(128)S(1)}, s32[128]{0:T(128)}, u32[]{:S(2)}) copy-start(s32[128]{0:T(128)} %param.8) | copy-start | bytes 1540
  20.1 4.4 %collective-permute-start.2 = (f32[256,1,128]{2,1,0:T(1,128)S(1)}, f32[256,1,128]{2,1,0:T(1,128)S(1)}, u32[]{:S(2)}, u32[]{:S(2)}) collective-permute-start(f32[256,1,128]{2,1,0:T(1,128)S(1)} %get-tuple-element.37), channel_id=1, source_target_pairs={{0,1},{1,2},{2,3},{3,0},{4,5},{5,6},{6,7},{7,4},{8,9},{9,10},{10,1... | collective-permute-start | bytes 393224 | tf_op jit(solution)/shard_map/ppermute | solution.py:20
  20.2 4.8 %collective-permute-start.3 = (f32[256,1,128]{2,1,0:T(1,128)S(1)}, f32[256,1,128]{2,1,0:T(1,128)S(1)}, u32[]{:S(2)}, u32[]{:S(2)}) collective-permute-start(f32[256,1,128]{2,1,0:T(1,128)S(1)} %get-tuple-element.38), channel_id=1, source_target_pairs={{1,0},{2,1},{3,2},{0,3},{5,4},{6,5},{7,6},{4,7},{9,8},{10,9},{11,1... | collective-permute-start | bytes 393224 | tf_op jit(solution)/shard_map/ppermute | solution.py:21
  26.2 12.4 %collective-permute-start.4 = (f32[1,128,512]{2,1,0:T(8,128)S(1)}, f32[1,128,512]{2,1,0:T(8,128)S(1)}, u32[]{:S(2)}, u32[]{:S(2)}) collective-permute-start(f32[1,128,512]{2,1,0:T(8,128)S(1)} %get-tuple-element.31), channel_id=1, source_target_pairs={{0,4},{4,8},{8,12},{12,16},{16,20},{20,24},{24,28},{28,0},{1,5},{5... | collective-permute-start | bytes 786440 | tf_op jit(solution)/shard_map/ppermute | solution.py:20
  26.5 15.0 %collective-permute-start.5 = (f32[1,128,512]{2,1,0:T(8,128)S(1)}, f32[1,128,512]{2,1,0:T(8,128)S(1)}, u32[]{:S(2)}, u32[]{:S(2)}) collective-permute-start(f32[1,128,512]{2,1,0:T(8,128)S(1)} %get-tuple-element.32), channel_id=1, source_target_pairs={{4,0},{8,4},{12,8},{16,12},{20,16},{24,20},{28,24},{0,28},{5,1},{9... | collective-permute-start | bytes 786440 | tf_op jit(solution)/shard_map/ppermute | solution.py:21
  43.4 4.4 %collective-permute-start.6 = (f32[256,1,128]{2,1,0:T(1,128)S(1)}, f32[256,1,128]{2,1,0:T(1,128)S(1)}, u32[]{:S(2)}, u32[]{:S(2)}) collective-permute-start(f32[256,1,128]{2,1,0:T(1,128)S(1)} %get-tuple-element.25), channel_id=1, source_target_pairs={{0,1},{1,2},{2,3},{3,0},{4,5},{5,6},{6,7},{7,4},{8,9},{9,10},{10,1... | collective-permute-start | bytes 393224 | tf_op jit(solution)/shard_map/ppermute | solution.py:20
  43.6 4.8 %collective-permute-start.7 = (f32[256,1,128]{2,1,0:T(1,128)S(1)}, f32[256,1,128]{2,1,0:T(1,128)S(1)}, u32[]{:S(2)}, u32[]{:S(2)}) collective-permute-start(f32[256,1,128]{2,1,0:T(1,128)S(1)} %get-tuple-element.26), channel_id=1, source_target_pairs={{1,0},{2,1},{3,2},{0,3},{5,4},{6,5},{7,6},{4,7},{9,8},{10,9},{11,1... | collective-permute-start | bytes 393224 | tf_op jit(solution)/shard_map/ppermute | solution.py:21
  48.9 0.7 copy-start.4
  87.5 30.8 %copy-start.2 = (f32[128]{0:T(128)S(1)}, f32[128]{0:T(128)}, u32[]{:S(2)}) copy-start(f32[128]{0:T(128)} %param.9) | copy-start | bytes 1540
where the time goes:
time: 150 us
  blocking collectives  72.1 us (48%)
  other arithmetic  27 us (18%)
  waiting for transfers between devices  26.6 us (18%)
  starting transfers between devices  14.5 us (10%)
  local copies, waits for them, and re-layouts  6.96 us (5%)
  matrix products  2.28 us (2%)
    all_gather x1, blocking collectives, per_device(): innovation = lax.all_gather(strip, 'row', axis=0, tiled=True)  30.8 us
    all_gather x1, blocking collectives, per_device(): lax.all_gather(sensor_horizontal_tile, 'row', axis=0, tiled=True)  30.7 us
    ppermute x4, waiting for transfers between devices, padded_2(): before = lax.ppermute(last, axis, up)  20.6 us
    another operation x3, other arithmetic, per_device(): factor = jnp.linalg.cholesky(innovation)  12.4 us
    ppermute x4, starting transfers between devices, padded_2(): after = lax.ppermute(initial, axis, down)  10.9 us
    another operation x2, other arithmetic, per_device(): jax.scipy.linalg.solve_triangular(factor, jnp.eye(station_total, dtype=jn...  10.5 us
    ppermute x4, waiting for transfers between devices, padded_2(): after = lax.ppermute(initial, axis, down)  5.97 us
    all_gather x1, blocking collectives, per_device(): lax.all_gather(tile_update_weighting, 'col', axis=1, tiled=True)  5.41 us
  transfers between devices with their start and end apart: 8, of which 8 were waited for; matrix products, arithmetic and copies ran while one was open for 0% of the time, Pallas kernels for 0%

commit v1 on v0

--- a/solution.py
+++ b/solution.py
@@ -1,6 +1,10 @@
+import functools
+
 import jax
 import jax.numpy as jnp
 from jax import lax
+from jax.experimental import pallas as pl
+from jax.experimental.pallas import tpu as pltpu
 from jax.sharding import PartitionSpec as P
 
 NC = 128
@@ -53,6 +57,215 @@
     extent_rows = surface.shape[0]
     doubled = jnp.concatenate([surface, surface], axis=0)
     return lax.dynamic_slice_in_dim(doubled, jnp.mod(offset, extent_rows), length, 0)
+
+
+def gather_kernel(
+    row_total, column_total, spread, row_sites, column_sites, gain, rows, innovation,
+    gain_all, rows_all, innovation_all,
+    gain_send, gain_recv, rows_send, rows_recv, innovation_send, innovation_recv,
+):
+    row = lax.axis_index("row")
+    column = lax.axis_index("col")
+    row_share, column_share = row_sites.shape[0], column_sites.shape[0]
+    barrier = pltpu.get_barrier_semaphore()
+    for step in range(1, column_total):
+        peer = lax.rem(column + step, column_total)
+        pl.semaphore_signal(barrier, 1, device_id={"col": peer}, device_id_type=pl.DeviceIdType.MESH)
+    for step in range(1, row_total):
+        peer = lax.rem(row + step, row_total)
+        pl.semaphore_signal(barrier, 1, device_id={"row": peer}, device_id_type=pl.DeviceIdType.MESH)
+
+    height, width = spread.shape
+    pick_rows = jnp.where(
+        row_sites[...] == lax.broadcasted_iota(jnp.int32, (row_share, height), 1), 1.0, 0.0
+    )
+    pick_columns = jnp.where(
+        column_sites[...] == lax.broadcasted_iota(jnp.int32, (column_share, width), 1), 1.0, 0.0
+    )
+
+    def gain_block(index):
+        return gain_all.at[pl.ds(pl.multiple_of(index * column_share, column_share), column_share)]
+
+    def rows_block(index):
+        return rows_all.at[pl.ds(pl.multiple_of(index * row_share, row_share), row_share)]
+
+    def innovation_block(index):
+        return innovation_all.at[pl.ds(pl.multiple_of(index * row_share, row_share), row_share)]
+
+    gain_block(column)[...] = lax.dot_general(
+        pick_columns, spread[...], (((1,), (1,)), ((), ())),
+        precision=finest_accuracy, preferred_element_type=jnp.float32,
+    )
+    rows_block(row)[...] = jnp.dot(
+        pick_rows, spread[...], precision=finest_accuracy, preferred_element_type=jnp.float32
+    )
+    pl.semaphore_wait(barrier, row_total + column_total - 2)
+
+    def exchange(block, me, axis, total, send, recv):
+        copies = []
+        for step in range(1, total):
+            peer = lax.rem(me + step, total)
+            copy = pltpu.make_async_remote_copy(
+                src_ref=block(me), dst_ref=block(me),
+                send_sem=send.at[step], recv_sem=recv.at[step],
+                device_id={axis: peer}, device_id_type=pl.DeviceIdType.MESH,
+            )
+            copy.start()
+            copies.append(copy)
+        return copies
+
+    def arrive(block, me, axis, total, send, recv):
+        for step in range(1, total):
+            source = lax.rem(me - step + total, total)
+            pltpu.make_async_remote_copy(
+                src_ref=block(source), dst_ref=block(source),
+                send_sem=send.at[step], recv_sem=recv.at[step],
+                device_id={axis: source}, device_id_type=pl.DeviceIdType.MESH,
+            ).wait_recv()
+
+    sent = exchange(gain_block, column, "col", column_total, gain_send, gain_recv)
+    sent += exchange(rows_block, row, "row", row_total, rows_send, rows_recv)
+    arrive(gain_block, column, "col", column_total, gain_send, gain_recv)
+    innovation_block(row)[...] = lax.dot_general(
+        pick_rows, gain_all[...], (((1,), (1,)), ((), ())),
+        precision=finest_accuracy, preferred_element_type=jnp.float32,
+    )
+    sent += exchange(innovation_block, row, "row", row_total, innovation_send, innovation_recv)
+    gain[...] = gain_all[...]
+    arrive(rows_block, row, "row", row_total, rows_send, rows_recv)
+    rows[...] = rows_all[...]
+    arrive(innovation_block, row, "row", row_total, innovation_send, innovation_recv)
+    innovation[...] = innovation_all[...]
+    for copy in sent:
+        copy.wait_send()
+
+
+def gather_call(spread, row_sites, column_sites, row_total, column_total):
+    height, width = spread.shape
+    stations = row_sites.shape[0] * row_total
+    shapes = [(stations, height), (stations, width), (stations, stations)]
+    vmem = pl.BlockSpec(memory_space=pltpu.VMEM)
+    semaphores = [pltpu.SemaphoreType.DMA((column_total,))] * 2
+    semaphores += [pltpu.SemaphoreType.DMA((row_total,))] * 4
+    return pl.pallas_call(
+        functools.partial(gather_kernel, row_total, column_total),
+        out_shape=[jax.ShapeDtypeStruct(shape, jnp.float32) for shape in shapes],
+        in_specs=[vmem] * 3,
+        out_specs=[vmem] * 3,
+        scratch_shapes=[pltpu.VMEM(shape, jnp.float32) for shape in shapes] + semaphores,
+        compiler_params=pltpu.CompilerParams(
+            collective_id=0, has_side_effects=True, vmem_limit_bytes=24 * 2**20
+        ),
+    )(spread, row_sites[:, None], column_sites[:, None])
+
+
+PIVOTS = 4
+
+
+def invert_block(d):
+    def mul(x, y):
+        return [[x[i][0] * y[0][j] + x[i][1] * y[1][j] for j in range(2)] for i in range(2)]
+
+    def inv(x):
+        scale = 1.0 / (x[0][0] * x[1][1] - x[0][1] * x[1][0])
+        return [[x[1][1] * scale, -x[0][1] * scale], [-x[1][0] * scale, x[0][0] * scale]]
+
+    def quarter(i, j):
+        return [[d[2 * i + a][2 * j + b] for b in range(2)] for a in range(2)]
+
+    def combine(x, y, sign):
+        return [[x[i][j] + sign * y[i][j] for j in range(2)] for i in range(2)]
+
+    e, f, g, h = quarter(0, 0), quarter(0, 1), quarter(1, 0), quarter(1, 1)
+    ei = inv(e)
+    eif, gei = mul(ei, f), mul(g, ei)
+    si = inv(combine(h, mul(g, eif), -1.0))
+    low = mul(si, gei)
+    upper = mul(eif, si)
+    first = combine(ei, mul(eif, low), 1.0)
+    return [
+        first[0] + [-upper[0][0], -upper[0][1]],
+        first[1] + [-upper[1][0], -upper[1][1]],
+        [-low[0][0], -low[0][1]] + si[0],
+        [-low[1][0], -low[1][1]] + si[1],
+    ]
+
+
+def invert(matrix):
+    n = matrix.shape[0]
+    group = 8
+    lanes = lax.broadcasted_iota(jnp.int32, (1, n), 1)
+    sublanes = lax.broadcasted_iota(jnp.int32, (group, n), 0)
+    parts = [matrix[i : i + group] for i in range(0, n, group)]
+    for first in range(0, n, PIVOTS):
+        home, at = first // group, first % group
+        columns = [
+            [jnp.broadcast_to(part[:, first + p : first + p + 1], (group, n)) for p in range(PIVOTS)]
+            for part in parts
+        ]
+        block = [
+            [columns[home][p][at + q : at + q + 1] for p in range(PIVOTS)] for q in range(PIVOTS)
+        ]
+        inverse = invert_block(block)
+        outside = jnp.where((lanes >= first) & (lanes < first + PIVOTS), 0.0, 1.0)
+        panel = [
+            jnp.where(lanes == first + q, 1.0, parts[home][at + q : at + q + 1] * outside)
+            for q in range(PIVOTS)
+        ]
+        solved = [
+            sum(inverse[q][p] * panel[p] for p in range(1, PIVOTS)) + inverse[q][0] * panel[0]
+            for q in range(PIVOTS)
+        ]
+        wide = [jnp.broadcast_to(row, (group, n)) for row in solved]
+        updated = []
+        for i, part in enumerate(parts):
+            terms = [columns[i][p] * wide[p] for p in range(PIVOTS)]
+            new = part * outside - ((terms[0] + terms[1]) + (terms[2] + terms[3]))
+            if i == home:
+                for q in range(PIVOTS):
+                    new = jnp.where(sublanes == at + q, wide[q], new)
+            updated.append(new)
+        parts = updated
+    return jnp.concatenate(parts, axis=0)
+
+
+def analysis_kernel(spread, innovation, noise, rows, gain, out):
+    stations = innovation.shape[0]
+    diagonal = lax.broadcasted_iota(jnp.int32, (stations, stations), 0) == lax.broadcasted_iota(
+        jnp.int32, (stations, stations), 1
+    )
+    matrix = innovation[...]
+    matrix = (matrix + matrix.T) * 0.5 + jnp.where(diagonal, noise[...], 0.0)
+    inverse = invert(matrix)
+    weighted = jnp.dot(
+        inverse, rows[...], precision=finest_accuracy, preferred_element_type=jnp.float32
+    )
+    out[...] = spread[...] - lax.dot_general(
+        gain[...], weighted, (((0,), (0,)), ((), ())),
+        precision=finest_accuracy, preferred_element_type=jnp.float32,
+    )
+
+
+def analysis_call(spread, innovation, noise, rows, gain):
+    stations = innovation.shape[0]
+    if stations > NC:
+        factor = jnp.linalg.cholesky(innovation + jnp.diag(noise))
+        inverse = jax.scipy.linalg.solve_triangular(
+            factor, jnp.eye(stations, dtype=jnp.float32), lower=True
+        )
+        left = jnp.dot(inverse, gain, precision=finest_accuracy)
+        right = jnp.dot(inverse, rows, precision=finest_accuracy)
+        return spread - lax.dot_general(
+            left, right, (((0,), (0,)), ((), ())), precision=finest_accuracy
+        )
+    vmem = pl.BlockSpec(memory_space=pltpu.VMEM)
+    return pl.pallas_call(
+        analysis_kernel,
+        out_shape=jax.ShapeDtypeStruct(spread.shape, jnp.float32),
+        in_specs=[vmem] * 5,
+        out_specs=vmem,
+        compiler_params=pltpu.CompilerParams(vmem_limit_bytes=24 * 2**20),
+    )(spread, innovation, noise[None, :], rows, gain)
 
 
 def per_device(covariance, courants, process_noise_spread, sensor_targets, noise_variance):
@@ -100,36 +313,10 @@
         lax.dynamic_slice_in_dim(sensor_targets, column_index * column_share, column_share)
         - column_index * vertical_tile_piece
     )
-    sensor_horizontal_tile = jnp.take(predicted_spread, sensor_horizontal_indices, axis=0)
-    tile_update_weighting = jnp.take(predicted_spread, sensor_vertical_indices, axis=1)
-    innovation_block = jnp.take(sensor_horizontal_tile, sensor_vertical_indices, axis=1)
-    strip = lax.all_gather(innovation_block, "col", axis=1, tiled=True)
-    innovation = lax.all_gather(strip, "row", axis=0, tiled=True)
-    innovation = innovation + jnp.diag(noise_variance)
-    factor = jnp.linalg.cholesky(innovation)
-    inverse = jax.scipy.linalg.solve_triangular(
-        factor, jnp.eye(station_total, dtype=jnp.float32), lower=True
-    )
-    columns = inverse
-    lower_triangle_target = jnp.dot(
-        columns,
-        lax.all_gather(sensor_horizontal_tile, "row", axis=0, tiled=True),
-        precision=finest_accuracy,
-    )
-    columns = inverse
-    lower_triangle_source = lax.dot_general(
-        columns,
-        lax.all_gather(tile_update_weighting, "col", axis=1, tiled=True),
-        (((1,), (1,)), ((), ())),
-        precision=finest_accuracy,
-    )
-    posterior_spread = predicted_spread - lax.dot_general(
-        lower_triangle_source,
-        lower_triangle_target,
-        (((0,), (0,)), ((), ())),
-        precision=finest_accuracy,
-    )
-    return posterior_spread
+    gain, rows, innovation = gather_call(
+        predicted_spread, sensor_horizontal_indices, sensor_vertical_indices, row_total, column_total
+    )
+    return analysis_call(predicted_spread, innovation, noise_variance, rows, gain)
 
 
 def solution(mesh):

time: 150 us -> 71.5 us (0.48)
  blocking collectives: 72.1 us -> 0 us
  other arithmetic: 27 us -> 3.74 us
  Pallas kernels: 0 us -> 20.9 us
  matrix products: 2.28 us -> 0 us
  local copies, waits for them, and re-layouts: 6.96 us -> 5.45 us
    all_gather x4 -> x0, blocking collectives: 72.1 us -> none  [the longest x1 30.8 us: per_device(): innovation = lax.all_gather(strip, 'row', axis=0, tiled=True)]
    another operation x5 -> x0, other arithmetic: 22.9 us -> none  [the longest x3 12.4 us: per_device(): factor = jnp.linalg.cholesky(innovation)]
    pallas_call x0 -> x2, Pallas kernels: none -> 20.9 us  [the longest x1 12.7 us: gather_call(): pl.pallas_call(functools.partial(gather_kernel, row_total, column_total),...]
    dot_general x3 -> x0, matrix products: 2.03 us -> none  [the longest x1 1.41 us: per_device(): lax.dot_general(lower_triangle_source, lower_triangle_target, (((0,), (0,...]
    gather x3 -> x0, local copies, waits for them, and re-layouts: 1.75 us -> none  [the longest x1 0.6 us: per_device(): jnp.take(predicted_spread, sensor_vertical_indices, axis=1)]
  transfers between devices with their start and end apart: 8 -> 8, of which waited for: 8 -> 8; matrix products, arithmetic and copies ran while one was open for 0% -> 1% of each run, Pallas kernels for 0% -> 0%
where the time goes in v1:
time: 71.5 us; the launch traced here: 71.3 us
  waiting for transfers between devices  26.4 us (37%)
  Pallas kernels  20.9 us (29%)
  starting transfers between devices  14.5 us (20%)
  local copies, waits for them, and re-layouts  5.45 us (8%)
  other arithmetic  3.74 us (5%)
    ppermute x4, waiting for transfers between devices, padded_2(): before = lax.ppermute(last, axis, up)  20.4 us
    pallas_call x1, Pallas kernels, gather_call(): pl.pallas_call(functools.partial(gather_kernel, row_total, column_total),...  12.7 us
    ppermute x4, starting transfers between devices, padded_2(): after = lax.ppermute(initial, axis, down)  10.9 us
    pallas_call x1, Pallas kernels, analysis_call(): pl.pallas_call(analysis_kernel, out_shape=jax.ShapeDtypeStruct(spread.sha...  8.15 us
    ppermute x4, waiting for transfers between devices, padded_2(): after = lax.ppermute(initial, axis, down)  5.97 us
    ppermute x4, starting transfers between devices, padded_2(): before = lax.ppermute(last, axis, up)  3.58 us
    slice x8, local copies, waits for them, and re-layouts, sweep_local(): jnp.roll(joint_spread_array, -1, which_axis)  2.87 us
    add x4, other arithmetic, sweep_local(): weight_behind * jnp.roll(joint_spread_array, 1, which_axis)  1.75 us
  transfers between devices with their start and end apart: 8, of which 8 were waited for; matrix products, arithmetic and copies ran while one was open for 1% of the time, Pallas kernels for 0%

profile of v1, /device:TPU:0, one launch (start us, length us, event | category | flops | bytes accessed | tf_op | source)
XLA Modules:
  0.0 71.3 jit_solution(1697171682793543418)
XLA Ops:
  0.0 1.4 %fusion.66 = (f32[2,127,512]{2,1,0:T(8,128)S(1)}, f32[2,127,512]{2,1,0:T(8,128)S(1)}) fusion(f32[2,128,512]{2,1,0:T(8,128)} %bitcast.19), kind=kLoop, calls=%fused_computation.123 | loop fusion | bytes 2080768 | tf_op jit(solution)/shard_map/jit(_roll_static)/slice | solution.py:43
  1.5 0.0 copy-done.2
  1.5 0.2 fusion.17
  1.8 3.0 %collective-permute-start = (f32[1,128,512]{2,1,0:T(8,128)S(1)}, f32[1,128,512]{2,1,0:T(8,128)S(1)}, u32[]{:S(2)}, u32[]{:S(2)}) collective-permute-start(f32[1,128,512]{2,1,0:T(8,128)S(1)} %get-tuple-element.45), channel_id=1, source_target_pairs={{0,4},{4,8},{8,12},{12,16},{16,20},{20,24},{24,28},{28,0},{1,5},{5... | collective-permute-start | bytes 786440 | tf_op jit(solution)/shard_map/ppermute | solution.py:24
  4.8 3.1 %collective-permute-start.1 = (f32[1,128,512]{2,1,0:T(8,128)S(1)}, f32[1,128,512]{2,1,0:T(8,128)S(1)}, u32[]{:S(2)}, u32[]{:S(2)}) collective-permute-start(f32[1,128,512]{2,1,0:T(8,128)S(1)} %get-tuple-element.46), channel_id=1, source_target_pairs={{4,0},{8,4},{12,8},{16,12},{20,16},{24,20},{28,24},{0,28},{5,1},{9... | collective-permute-start | bytes 786440 | tf_op jit(solution)/shard_map/ppermute | solution.py:25
  8.1 7.9 %collective-permute-done = f32[1,128,512]{2,1,0:T(8,128)S(1)} collective-permute-done((f32[1,128,512]{2,1,0:T(8,128)S(1)}, f32[1,128,512]{2,1,0:T(8,128)S(1)}, u32[]{:S(2)}, u32[]{:S(2)}) %collective-permute-start) | collective-permute-done | bytes 262176 | tf_op jit(solution)/shard_map/ppermute | solution.py:24
  16.0 2.2 %collective-permute-done.1 = f32[1,128,512]{2,1,0:T(8,128)S(1)} collective-permute-done((f32[1,128,512]{2,1,0:T(8,128)S(1)}, f32[1,128,512]{2,1,0:T(8,128)S(1)}, u32[]{:S(2)}, u32[]{:S(2)}) %collective-permute-start.1) | collective-permute-done | bytes 262176 | tf_op jit(solution)/shard_map/ppermute | solution.py:25
  18.2 0.2 fusion.13
  18.3 0.2 reshape.114
  18.5 0.3 fusion.63
  18.9 0.3 fusion.64
  19.2 0.7 fusion.19
  19.9 0.2 fusion.62
  20.1 0.1 collective-permute-start.2
  20.2 1.7 %collective-permute-start.3 = (f32[256,1,128]{2,1,0:T(1,128)S(1)}, f32[256,1,128]{2,1,0:T(1,128)S(1)}, u32[]{:S(2)}, u32[]{:S(2)}) collective-permute-start(f32[256,1,128]{2,1,0:T(1,128)S(1)} %get-tuple-element.40), channel_id=1, source_target_pairs={{1,0},{2,1},{3,2},{0,3},{5,4},{6,5},{7,6},{4,7},{9,8},{10,9},{11,1... | collective-permute-start | bytes 393224 | tf_op jit(solution)/shard_map/ppermute | solution.py:25
  21.9 2.6 %collective-permute-done.2 = f32[256,1,128]{2,1,0:T(1,128)S(1)} collective-permute-done((f32[256,1,128]{2,1,0:T(1,128)S(1)}, f32[256,1,128]{2,1,0:T(1,128)S(1)}, u32[]{:S(2)}, u32[]{:S(2)}) %collective-permute-start.2) | collective-permute-done | bytes 131104 | tf_op jit(solution)/shard_map/ppermute | solution.py:24
  24.6 0.4 collective-permute-done.3
  25.0 0.6 fusion.9
  25.6 0.2 reshape.115
  25.8 0.1 fusion.60
  25.9 0.2 fusion.21
  26.1 0.0 copy-start.3
  26.2 0.3 collective-permute-start.4
  26.5 4.4 %collective-permute-start.5 = (f32[1,128,512]{2,1,0:T(8,128)S(1)}, f32[1,128,512]{2,1,0:T(8,128)S(1)}, u32[]{:S(2)}, u32[]{:S(2)}) collective-permute-start(f32[1,128,512]{2,1,0:T(8,128)S(1)} %get-tuple-element.34), channel_id=1, source_target_pairs={{4,0},{8,4},{12,8},{16,12},{20,16},{24,20},{28,24},{0,28},{5,1},{9... | collective-permute-start | bytes 786440 | tf_op jit(solution)/shard_map/ppermute | solution.py:25
  30.9 0.1 subtract_bitcast_fusion.1
  31.0 7.6 %collective-permute-done.4 = f32[1,128,512]{2,1,0:T(8,128)S(1)} collective-permute-done((f32[1,128,512]{2,1,0:T(8,128)S(1)}, f32[1,128,512]{2,1,0:T(8,128)S(1)}, u32[]{:S(2)}, u32[]{:S(2)}) %collective-permute-start.4) | collective-permute-done | bytes 262176 | tf_op jit(solution)/shard_map/ppermute | solution.py:24
  38.6 2.9 %collective-permute-done.5 = f32[1,128,512]{2,1,0:T(8,128)S(1)} collective-permute-done((f32[1,128,512]{2,1,0:T(8,128)S(1)}, f32[1,128,512]{2,1,0:T(8,128)S(1)}, u32[]{:S(2)}, u32[]{:S(2)}) %collective-permute-start.5) | collective-permute-done | bytes 262176 | tf_op jit(solution)/shard_map/ppermute | solution.py:25
  41.5 0.2 fusion.5
  41.6 0.2 reshape.116
  41.8 0.3 fusion.57
  42.2 0.3 fusion.58
  42.5 0.7 fusion.23
  43.2 0.2 fusion.56
  43.4 0.2 collective-permute-start.6
  43.6 1.6 %collective-permute-start.7 = (f32[256,1,128]{2,1,0:T(1,128)S(1)}, f32[256,1,128]{2,1,0:T(1,128)S(1)}, u32[]{:S(2)}, u32[]{:S(2)}) collective-permute-start(f32[256,1,128]{2,1,0:T(1,128)S(1)} %get-tuple-element.28), channel_id=1, source_target_pairs={{1,0},{2,1},{3,2},{0,3},{5,4},{6,5},{7,6},{4,7},{9,8},{10,9},{11,1... | collective-permute-start | bytes 393224 | tf_op jit(solution)/shard_map/ppermute | solution.py:25
  45.2 0.1 subtract_bitcast_fusion
  45.3 0.1 copy.7.column_sites
  45.4 0.1 copy.6.row_sites
  45.5 2.4 %collective-permute-done.6 = f32[256,1,128]{2,1,0:T(1,128)S(1)} collective-permute-done((f32[256,1,128]{2,1,0:T(1,128)S(1)}, f32[256,1,128]{2,1,0:T(1,128)S(1)}, u32[]{:S(2)}, u32[]{:S(2)}) %collective-permute-start.6) | collective-permute-done | bytes 131104 | tf_op jit(solution)/shard_map/ppermute | solution.py:24
  47.9 0.5 collective-permute-done.7
  48.3 0.6 fusion.1
  48.9 0.0 copy-start.4
  48.9 0.7 copy-done.4
  49.6 0.1 bitcast_add_fusion.spread
  49.8 12.7 %shard_map.55 = (f32[128,256]{1,0:T(8,128)S(1)}, f32[128,512]{1,0:T(8,128)S(1)}, f32[128,128]{1,0:T(8,128)S(1)}) custom-call(f32[256,512]{1,0:T(8,128)S(1)} %bitcast_add_fusion.spread, s32[16,1]{1,0:T(8,128)S(1)} %copy.6.row_sites, s32[32,1]{1,0:T(8,128)S(1)} %copy.7.column_sites), custom_call_target="tpu_custom_call" | custom-call | tf_op jit(solution)/shard_map/pallas_call | solution.py:150
  62.5 0.0 copy-start
  62.5 0.6 copy-done
  63.1 8.2 %shard_map.56 = f32[256,512]{1,0:T(8,128)} custom-call(f32[256,512]{1,0:T(8,128)S(1)} %bitcast_add_fusion.spread, f32[128,128]{1,0:T(8,128)S(1)} %get-tuple-element.8.innovation, f32[1,128]{1,0:T(1,128)S(1)} %bitcast.18, f32[128,512]{1,0:T(8,128)S(1)} %get-tuple-element.9.rows, f32[128,256]{1,0:T(8,128)S(1)} %get-tuple-element.10.gain), custom_call_target="tpu_custom_call" | custom-call | tf_op jit(solution)/shard_map/pallas_call | solution.py:262
  (27 shorter events, 0.3 us)
Async XLA Ops:
  0.0 1.4 %copy-start.1 = (f32[256,512]{1,0:T(8,128)S(1)}, f32[256,512]{1,0:T(8,128)}, u32[]{:S(2)}) copy-start(f32[256,512]{1,0:T(8,128)} %param.5) | copy-start | bytes 1572868
  0.0 1.5 %copy-start.2 = (f32[2,2,16,128]{3,2,1,0:T(8,128)S(1)}, f32[2,2,16,128]{3,2,1,0:T(8,128)}, u32[]{:S(2)}) copy-start(f32[2,2,16,128]{3,2,1,0:T(8,128)} %param.6) | copy-start | bytes 98308
  1.8 14.2 %collective-permute-start = (f32[1,128,512]{2,1,0:T(8,128)S(1)}, f32[1,128,512]{2,1,0:T(8,128)S(1)}, u32[]{:S(2)}, u32[]{:S(2)}) collective-permute-start(f32[1,128,512]{2,1,0:T(8,128)S(1)} %get-tuple-element.45), channel_id=1, source_target_pairs={{0,4},{4,8},{8,12},{12,16},{16,20},{20,24},{24,28},{28,0},{1,5},{5... | collective-permute-start | bytes 786440 | tf_op jit(solution)/shard_map/ppermute | solution.py:24
  4.8 13.4 %collective-permute-start.1 = (f32[1,128,512]{2,1,0:T(8,128)S(1)}, f32[1,128,512]{2,1,0:T(8,128)S(1)}, u32[]{:S(2)}, u32[]{:S(2)}) collective-permute-start(f32[1,128,512]{2,1,0:T(8,128)S(1)} %get-tuple-element.46), channel_id=1, source_target_pairs={{4,0},{8,4},{12,8},{16,12},{20,16},{24,20},{28,24},{0,28},{5,1},{9... | collective-permute-start | bytes 786440 | tf_op jit(solution)/shard_map/ppermute | solution.py:25
  20.1 4.4 %collective-permute-start.2 = (f32[256,1,128]{2,1,0:T(1,128)S(1)}, f32[256,1,128]{2,1,0:T(1,128)S(1)}, u32[]{:S(2)}, u32[]{:S(2)}) collective-permute-start(f32[256,1,128]{2,1,0:T(1,128)S(1)} %get-tuple-element.39), channel_id=1, source_target_pairs={{0,1},{1,2},{2,3},{3,0},{4,5},{5,6},{6,7},{7,4},{8,9},{9,10},{10,1... | collective-permute-start | bytes 393224 | tf_op jit(solution)/shard_map/ppermute | solution.py:24
  20.2 4.8 %collective-permute-start.3 = (f32[256,1,128]{2,1,0:T(1,128)S(1)}, f32[256,1,128]{2,1,0:T(1,128)S(1)}, u32[]{:S(2)}, u32[]{:S(2)}) collective-permute-start(f32[256,1,128]{2,1,0:T(1,128)S(1)} %get-tuple-element.40), channel_id=1, source_target_pairs={{1,0},{2,1},{3,2},{0,3},{5,4},{6,5},{7,6},{4,7},{9,8},{10,9},{11,1... | collective-permute-start | bytes 393224 | tf_op jit(solution)/shard_map/ppermute | solution.py:25
  26.1 4.8 %copy-start.3 = (s32[128]{0:T(128)S(1)}, s32[128]{0:T(128)}, u32[]{:S(2)}) copy-start(s32[128]{0:T(128)} %param.8) | copy-start | bytes 1540
  26.2 12.4 %collective-permute-start.4 = (f32[1,128,512]{2,1,0:T(8,128)S(1)}, f32[1,128,512]{2,1,0:T(8,128)S(1)}, u32[]{:S(2)}, u32[]{:S(2)}) collective-permute-start(f32[1,128,512]{2,1,0:T(8,128)S(1)} %get-tuple-element.33), channel_id=1, source_target_pairs={{0,4},{4,8},{8,12},{12,16},{16,20},{20,24},{24,28},{28,0},{1,5},{5... | collective-permute-start | bytes 786440 | tf_op jit(solution)/shard_map/ppermute | solution.py:24
  26.5 15.0 %collective-permute-start.5 = (f32[1,128,512]{2,1,0:T(8,128)S(1)}, f32[1,128,512]{2,1,0:T(8,128)S(1)}, u32[]{:S(2)}, u32[]{:S(2)}) collective-permute-start(f32[1,128,512]{2,1,0:T(8,128)S(1)} %get-tuple-element.34), channel_id=1, source_target_pairs={{4,0},{8,4},{12,8},{16,12},{20,16},{24,20},{28,24},{0,28},{5,1},{9... | collective-permute-start | bytes 786440 | tf_op jit(solution)/shard_map/ppermute | solution.py:25
  43.4 4.4 %collective-permute-start.6 = (f32[256,1,128]{2,1,0:T(1,128)S(1)}, f32[256,1,128]{2,1,0:T(1,128)S(1)}, u32[]{:S(2)}, u32[]{:S(2)}) collective-permute-start(f32[256,1,128]{2,1,0:T(1,128)S(1)} %get-tuple-element.27), channel_id=1, source_target_pairs={{0,1},{1,2},{2,3},{3,0},{4,5},{5,6},{6,7},{7,4},{8,9},{9,10},{10,1... | collective-permute-start | bytes 393224 | tf_op jit(solution)/shard_map/ppermute | solution.py:24
  43.6 4.8 %collective-permute-start.7 = (f32[256,1,128]{2,1,0:T(1,128)S(1)}, f32[256,1,128]{2,1,0:T(1,128)S(1)}, u32[]{:S(2)}, u32[]{:S(2)}) collective-permute-start(f32[256,1,128]{2,1,0:T(1,128)S(1)} %get-tuple-element.28), channel_id=1, source_target_pairs={{1,0},{2,1},{3,2},{0,3},{5,4},{6,5},{7,6},{4,7},{9,8},{10,9},{11,1... | collective-permute-start | bytes 393224 | tf_op jit(solution)/shard_map/ppermute | solution.py:25
  48.9 0.7 copy-start.4
  62.5 0.7 copy-start

commit v2 on v1

--- a/solution.py
+++ b/solution.py
@@ -14,49 +14,194 @@
 finest_accuracy = lax.Precision.HIGHEST
 
 
-def padded_2(array, sides, width):
-    for axis, dim in sides:
-        size, length = (lax.axis_size(axis), array.shape[dim])
-        up = [(i, (i + 1) % size) for i in range(size)]
-        down = [(j, i) for i, j in up]
-        last = lax.slice_in_dim(array, length - width, length, axis=dim)
-        initial = lax.slice_in_dim(array, 0, width, axis=dim)
-        before = lax.ppermute(last, axis, up)
-        after = lax.ppermute(initial, axis, down)
-        array = jnp.concatenate([before, array, after], axis=dim)
-    return array
-
-
-def stencil_weights(courant):
-    return (
-        courant * (1.0 + courant) * 0.5,
-        1.0 - courant * courant,
-        courant * (courant - 1.0) * 0.5,
-    )
-
-
-def sweep_local(joint_spread_array, courant, which_axis):
-    weight_behind, weight_centre, weight_ahead = stencil_weights(courant)
-    return (
-        weight_behind * jnp.roll(joint_spread_array, 1, which_axis)
-        + weight_centre * joint_spread_array
-        + weight_ahead * jnp.roll(joint_spread_array, -1, which_axis)
-    )
-
-
-def sweep_padded(padded, courant, which_axis, keep_rows):
-    weight_behind, weight_centre, weight_ahead = stencil_weights(courant)
-    lower_rows = lax.slice_in_dim(padded, 0, keep_rows, axis=which_axis)
-    middle = lax.slice_in_dim(padded, 1, keep_rows + 1, axis=which_axis)
-    upper_rows = lax.slice_in_dim(padded, 2, keep_rows + 2, axis=which_axis)
-    return weight_behind * lower_rows + weight_centre * middle + weight_ahead * upper_rows
-
-
-def wind_rows(courants, cycle_index, component, offset, length):
-    surface = courants[cycle_index, component]
-    extent_rows = surface.shape[0]
-    doubled = jnp.concatenate([surface, surface], axis=0)
-    return lax.dynamic_slice_in_dim(doubled, jnp.mod(offset, extent_rows), length, 0)
+def sweep(behind, centre, ahead, courant):
+    total = None
+    for value, weight in (
+        (behind, lambda: courant * (1.0 + courant) * 0.5),
+        (centre, lambda: 1.0 - courant * courant),
+        (ahead, lambda: courant * (courant - 1.0) * 0.5),
+    ):
+        if value is not None:
+            term = weight() * value
+            total = term if total is None else total + term
+    return total
+
+
+def advance(stack, winds, axis):
+    length = NC
+    for cycle in range(CYCLES):
+        stack = [
+            None if line is None else sweep(
+                pltpu.roll(line, 1, axis), line, pltpu.roll(line, length - 1, axis),
+                winds(cycle, 0, cycle + at),
+            )
+            for at, line in enumerate(stack)
+        ]
+        stack = [
+            sweep(stack[at - 1], stack[at], stack[at + 1], winds(cycle, 1, cycle + at))
+            for at in range(1, len(stack) - 1)
+        ]
+    return stack
+
+
+def forecast_kernel(
+    row_total, column_total, covariance, courants, noise, out,
+    wind, done, travelled, term, arrived, behind, ahead,
+    far_send, far_recv, near_send, near_recv, behind_send, behind_recv, ahead_send, ahead_recv,
+):
+    row = lax.axis_index("row")
+    column = lax.axis_index("col")
+    height, width = covariance.shape
+    band_rows, band_columns = height // NC, width // NC
+    grid_rows = courants.shape[2]
+    half = lax.rem(row, 2)
+    partner = row + 1 - 2 * half
+    far_target = lax.rem(row + 4 * half - 2 + row_total, row_total)
+    far_source = lax.rem(row + 2 - 4 * half + row_total, row_total)
+    before = lax.rem(column + column_total - 1, column_total)
+    after = lax.rem(column + 1, column_total)
+    mesh_id = pl.DeviceIdType.MESH
+
+    barrier = pltpu.get_barrier_semaphore()
+    for peer in (far_target, far_source, partner):
+        pl.semaphore_signal(barrier, 1, device_id={"row": peer}, device_id_type=mesh_id)
+    for peer in (before, after):
+        pl.semaphore_signal(barrier, 1, device_id={"col": peer}, device_id_type=mesh_id)
+    pl.semaphore_wait(barrier, 5)
+
+    def chunk(k):
+        return covariance.at[:, k * NC : (k + 1) * NC]
+
+    def copy(source, target, send, recv, at, axis, peer):
+        return pltpu.make_async_remote_copy(
+            src_ref=source, dst_ref=target, send_sem=send.at[at], recv_sem=recv.at[at],
+            device_id={axis: peer}, device_id_type=mesh_id,
+        )
+
+    far = [
+        copy(chunk(k), travelled.at[k], far_send, far_recv, k, "row", far_target)
+        for k in range(band_columns)
+    ]
+    for transfer in far:
+        transfer.start()
+
+    window = 2 * band_rows + 2 * CYCLES
+    pair_first = (row - half) * band_rows - CYCLES + grid_rows
+    for cycle in range(CYCLES):
+        for component in range(2):
+            for at in range(window):
+                line = courants[
+                    cycle, component, pl.ds(lax.rem(pair_first + at, grid_rows), 1), :
+                ]
+                wind[cycle, component, at] = jnp.broadcast_to(line, (NC, NC)).T
+
+    def winds_of(offset):
+        return lambda cycle, component, at: wind[cycle, component, offset + at]
+
+    own_offset = half * band_rows
+    other_offset = band_rows - own_offset
+
+    def own_part(k, _):
+        columns = pl.ds(pl.multiple_of(k * NC, NC), NC)
+        own = [covariance[i * NC : (i + 1) * NC, columns] for i in range(band_rows)]
+        lines = advance([None] * CYCLES + own + [None] * CYCLES, winds_of(own_offset), 0)
+        for i, line in enumerate(lines):
+            done[k, i * NC : (i + 1) * NC, :] = line
+        return 0
+
+    lax.fori_loop(0, band_columns, own_part, 0)
+
+    near = [
+        copy(term.at[k], arrived.at[k], near_send, near_recv, k, "row", partner)
+        for k in range(band_columns)
+    ]
+    sides = []
+
+    def finish(k):
+        near[k].wait_recv()
+        done[k] = done[k] + arrived[k]
+        if k < CYCLES:
+            sides.append(copy(done.at[k], ahead.at[k], ahead_send, ahead_recv, k, "col", before))
+            sides[-1].start()
+        if k >= band_columns - CYCLES:
+            at = k - (band_columns - CYCLES)
+            sides.append(copy(done.at[k], behind.at[at], behind_send, behind_recv, at, "col", after))
+            sides[-1].start()
+
+    for k in range(band_columns):
+        far[k].wait_recv()
+        lower, upper = [], []
+        for i in range(band_rows):
+            rows = slice(i * NC, (i + 1) * NC)
+            own, other = covariance[rows, k * NC : (k + 1) * NC], travelled[k, rows, :]
+            lower.append(jnp.where(half == 1, other, own))
+            upper.append(jnp.where(half == 1, own, other))
+        lines = advance(lower + [None] * band_rows + upper, winds_of(other_offset), 0)
+        for i, line in enumerate(lines):
+            term[k, i * NC : (i + 1) * NC, :] = line
+        near[k].start()
+        if k:
+            finish(k - 1)
+    finish(band_columns - 1)
+    for transfer in sides:
+        transfer.wait_recv()
+
+    column_first = column * band_columns - CYCLES + grid_rows
+    column_winds = {
+        (cycle, component, at): courants[
+            cycle, component, pl.ds(lax.rem(column_first + at, grid_rows), 1), :
+        ]
+        for cycle in range(CYCLES)
+        for component in range(2)
+        for at in range(band_columns + 2 * CYCLES)
+    }
+    step = 32
+    for i in range(band_rows):
+        cell_noise = noise[i : i + 1, :]
+
+        def piece(m, _):
+            first = pl.multiple_of(m * step, step)
+            rows = pl.ds(i * NC + first, step)
+            stack = [behind[k, rows, :] for k in range(CYCLES)]
+            stack += [done[k, rows, :] for k in range(band_columns)]
+            stack += [ahead[k, rows, :] for k in range(CYCLES)]
+            lines = advance(stack, lambda *key: column_winds[key], 1)
+            matches = first + lax.broadcasted_iota(
+                jnp.int32, (step, NC), 0
+            ) == lax.broadcasted_iota(jnp.int32, (step, NC), 1)
+            for k, line in enumerate(lines):
+                here = row * band_rows + i == column * band_columns + k
+                extra = jnp.where(matches & here, cell_noise, 0.0)
+                out[rows, k * NC : (k + 1) * NC] = line + extra
+            return 0
+
+        lax.fori_loop(0, NC // step, piece, 0)
+
+    for transfer in far + near + sides:
+        transfer.wait_send()
+
+
+def forecast_call(covariance, courants, noise, row_total, column_total):
+    height, width = covariance.shape
+    band_rows, band_columns = height // NC, width // NC
+    vmem = pl.BlockSpec(memory_space=pltpu.VMEM)
+    lines = pltpu.VMEM((band_columns, height, NC), jnp.float32)
+    side = pltpu.VMEM((CYCLES, height, NC), jnp.float32)
+    window = 2 * band_rows + 2 * CYCLES
+    return pl.pallas_call(
+        functools.partial(forecast_kernel, row_total, column_total),
+        out_shape=jax.ShapeDtypeStruct(covariance.shape, jnp.float32),
+        in_specs=[vmem] * 3,
+        out_specs=vmem,
+        scratch_shapes=[pltpu.VMEM((CYCLES, 2, window, NC, NC), jnp.float32)]
+        + [lines] * 4
+        + [side] * 2
+        + [pltpu.SemaphoreType.DMA((band_columns,))] * 4
+        + [pltpu.SemaphoreType.DMA((CYCLES,))] * 4,
+        compiler_params=pltpu.CompilerParams(
+            collective_id=1, has_side_effects=True, vmem_limit_bytes=24 * 2**20
+        ),
+    )(covariance, courants, noise)
 
 
 def gather_kernel(
@@ -274,33 +419,8 @@
     row_total = lax.axis_size("row")
     column_total = lax.axis_size("col")
     horizontal_tile_piece, vertical_tile_piece = covariance.shape
-    band_rows = horizontal_tile_piece // NC
-    band_columns = vertical_tile_piece // NC
-    row_first = row_index * band_rows
-    column_first = column_index * band_columns
-    joint_spread_array = covariance
-    for cycle_index in range(CYCLES):
-        joint_spread_array = joint_spread_array.reshape(band_rows, NC, vertical_tile_piece)
-        eastward = wind_rows(courants, cycle_index, 0, row_first, band_rows)[:, :, None]
-        joint_spread_array = sweep_local(joint_spread_array, eastward, 1)
-        padded = padded_2(joint_spread_array, (("row", 0),), 1)
-        northward = wind_rows(courants, cycle_index, 1, row_first, band_rows)[:, :, None]
-        joint_spread_array = sweep_padded(padded, northward, 0, band_rows)
-        joint_spread_array = joint_spread_array.reshape(horizontal_tile_piece, band_columns, NC)
-        eastward = wind_rows(courants, cycle_index, 0, column_first, band_columns)[None]
-        joint_spread_array = sweep_local(joint_spread_array, eastward, 2)
-        padded = padded_2(joint_spread_array, (("col", 1),), 1)
-        northward = wind_rows(courants, cycle_index, 1, column_first, band_columns)[None]
-        joint_spread_array = sweep_padded(padded, northward, 1, band_columns)
-    predicted_spread = joint_spread_array.reshape(horizontal_tile_piece, vertical_tile_piece)
-    row_ids = row_index * horizontal_tile_piece + jnp.arange(horizontal_tile_piece, dtype=jnp.int32)
-    column_ids = column_index * vertical_tile_piece + jnp.arange(
-        vertical_tile_piece, dtype=jnp.int32
-    )
-    predicted_spread = predicted_spread + jnp.where(
-        row_ids[:, None] == column_ids[None, :],
-        process_noise_spread.reshape(horizontal_tile_piece, 1),
-        0.0,
+    predicted_spread = forecast_call(
+        covariance, courants, process_noise_spread, row_total, column_total
     )
     station_total = sensor_targets.shape[0]
     row_share = station_total // row_total

time: 71.5 us -> 51.8 us (0.72)
  Pallas kernels: 20.9 us -> 47.6 us
  waiting for transfers between devices: 26.4 us -> 0 us
  starting transfers between devices: 14.5 us -> 0 us
  local copies, waits for them, and re-layouts: 5.45 us -> 2.46 us
  other arithmetic: 3.74 us -> 1.46 us
    pallas_call x0 -> x1, Pallas kernels: none -> 28.2 us  [forecast_call(): pl.pallas_call(functools.partial(forecast_kernel, row_total, column_total...]
    ppermute x8 -> x0, waiting for transfers between devices: 26.4 us -> none  [the longest x4 20.4 us: padded_2(): before = lax.ppermute(last, axis, up)]
    ppermute x8 -> x0, starting transfers between devices: 14.5 us -> none  [the longest x4 10.9 us: padded_2(): after = lax.ppermute(initial, axis, down)]
    add x11 -> x0, other arithmetic: 3.4 us -> none  [the longest x4 1.75 us: sweep_local(): weight_behind * jnp.roll(joint_spread_array, 1, which_axis)]
    slice x12 -> x0, local copies, waits for them, and re-layouts: 3.35 us -> none  [the longest x8 2.87 us: sweep_local(): jnp.roll(joint_spread_array, -1, which_axis)]
    pallas_call x1, Pallas kernels: 12.7 us -> 11.3 us  [gather_call(): pl.pallas_call(functools.partial(gather_kernel, row_total, column_total),...]
    unnamed x10 -> x8, local copies, waits for them, and re-layouts: 1.34 us -> 2.28 us
  transfers between devices with their start and end apart: 8 -> 0, of which waited for: 8 -> 0; matrix products, arithmetic and copies ran while one was open for 1% -> 0% of each run, Pallas kernels for 0% -> 0%
where the time goes in v2:
time: 51.8 us; the launch traced here: 51.5 us
  Pallas kernels  47.6 us (92%)
  local copies, waits for them, and re-layouts  2.46 us (5%)
  other arithmetic  1.46 us (3%)
    pallas_call x1, Pallas kernels, forecast_call(): pl.pallas_call(functools.partial(forecast_kernel, row_total, column_total...  28.2 us
    pallas_call x1, Pallas kernels, gather_call(): pl.pallas_call(functools.partial(gather_kernel, row_total, column_total),...  11.3 us
    pallas_call x1, Pallas kernels, analysis_call(): pl.pallas_call(analysis_kernel, out_shape=jax.ShapeDtypeStruct(spread.sha...  8.16 us
    unnamed x8, local copies, waits for them, and re-layouts  2.28 us

profile of v2, /device:TPU:0, one launch (start us, length us, event | category | flops | bytes accessed | tf_op | source)
XLA Modules:
  0.0 51.5 jit_solution(17254054401472327717)
XLA Ops:
  0.0 0.0 copy-start.1
  0.0 0.7 %subtract_bitcast_fusion = s32[32,1]{0,1:T(1,128)S(1)} fusion(s32[128]{0:T(128)} %param.8, s32[]{:T(128)S(6)} %select_n.7, s32[]{:T(128)S(6)} %mul.15), kind=kLoop, calls=%fused_computation | loop fusion | flops 32 | bytes 264 | tf_op jit(solution)/shard_map/broadcast_in_dim | solution.py:304
  0.7 0.7 %subtract_bitcast_fusion.1 = s32[16,1]{0,1:T(1,128)S(1)} fusion(s32[128]{0:T(128)} %param.8, s32[]{:T(128)S(6)} %select_n.6, s32[]{:T(128)S(6)} %mul.13), kind=kLoop, calls=%fused_computation.1 | loop fusion | flops 16 | bytes 136 | tf_op jit(solution)/shard_map/broadcast_in_dim | solution.py:304
  1.5 0.1 copy.6.row_sites
  1.6 0.0 copy-start.2
  1.6 0.1 copy.7.column_sites
  1.6 0.0 copy-done.1
  1.6 0.6 %copy-done.2 = f32[2,128]{1,0:T(2,128)S(1)} copy-done((f32[2,128]{1,0:T(2,128)S(1)}, f32[2,128]{1,0:T(2,128)}, u32[]{:S(2)}) %copy-start.2) | copy-done | bytes 1048
  2.2 0.0 copy-start
  2.2 1.0 %copy-done = f32[256,512]{1,0:T(8,128)S(1)} copy-done((f32[256,512]{1,0:T(8,128)S(1)}, f32[256,512]{1,0:T(8,128)}, u32[]{:S(2)}) %copy-start) | copy-done | bytes 524312
  3.3 28.2 %shard_map.55.spread = f32[256,512]{1,0:T(8,128)S(1)} custom-call(f32[256,512]{1,0:T(8,128)S(1)} %copy-done, f32[2,2,16,128]{3,2,1,0:T(8,128)S(1)} %copy-done.1, f32[2,128]{1,0:T(2,128)S(1)} %copy-done.2), custom_call_target="tpu_custom_call" | custom-call | tf_op jit(solution)/shard_map/pallas_call | solution.py:191
  31.4 11.3 %shard_map.56 = (f32[128,256]{1,0:T(8,128)S(1)}, f32[128,512]{1,0:T(8,128)S(1)}, f32[128,128]{1,0:T(8,128)S(1)}) custom-call(f32[256,512]{1,0:T(8,128)S(1)} %shard_map.55.spread, s32[16,1]{1,0:T(8,128)S(1)} %copy.6.row_sites, s32[32,1]{1,0:T(8,128)S(1)} %copy.7.column_sites), custom_call_target="tpu_custom_call" | custom-call | tf_op jit(solution)/shard_map/pallas_call | solution.py:295
  42.7 0.0 copy-start.3
  42.7 0.6 %copy-done.3 = f32[128]{0:T(128)S(1)} copy-done((f32[128]{0:T(128)S(1)}, f32[128]{0:T(128)}, u32[]{:S(2)}) %copy-start.3) | copy-done | bytes 536
  43.4 8.2 %shard_map.57 = f32[256,512]{1,0:T(8,128)} custom-call(f32[256,512]{1,0:T(8,128)S(1)} %shard_map.55.spread, f32[128,128]{1,0:T(8,128)S(1)} %get-tuple-element.8.innovation, f32[1,128]{1,0:T(1,128)S(1)} %bitcast.5, f32[128,512]{1,0:T(8,128)S(1)} %get-tuple-element.9.rows, f32[128,256]{1,0:T(8,128)S(1)} %get-tuple-element.10.gain), custom_call_target="tpu_custom_call" | custom-call | tf_op jit(solution)/shard_map/pallas_call | solution.py:407
Async XLA Ops:
  0.0 1.6 %copy-start.1 = (f32[2,2,16,128]{3,2,1,0:T(8,128)S(1)}, f32[2,2,16,128]{3,2,1,0:T(8,128)}, u32[]{:S(2)}) copy-start(f32[2,2,16,128]{3,2,1,0:T(8,128)} %courants.1) | copy-start | bytes 98308
  1.6 0.7 %copy-start.2 = (f32[2,128]{1,0:T(2,128)S(1)}, f32[2,128]{1,0:T(2,128)}, u32[]{:S(2)}) copy-start(f32[2,128]{1,0:T(2,128)} %noise.1) | copy-start | bytes 3076
  2.2 1.0 %copy-start = (f32[256,512]{1,0:T(8,128)S(1)}, f32[256,512]{1,0:T(8,128)}, u32[]{:S(2)}) copy-start(f32[256,512]{1,0:T(8,128)} %covariance.1) | copy-start | bytes 1572868
  42.7 0.7 %copy-start.3 = (f32[128]{0:T(128)S(1)}, f32[128]{0:T(128)}, u32[]{:S(2)}) copy-start(f32[128]{0:T(128)} %param.9) | copy-start | bytes 1540

commit v3 on v2

--- a/solution.py
+++ b/solution.py
@@ -45,9 +45,12 @@
 
 
 def forecast_kernel(
-    row_total, column_total, covariance, courants, noise, out,
-    wind, done, travelled, term, arrived, behind, ahead,
+    row_total, column_total, covariance_in, courants_in, noise_in, targets_in, variance_in,
+    out, gain_out, rows_out, innovation_out,
+    covariance, courants, noise, targets, variance, sites, gain_all, rows_all, innovation_all,
+    wind, done, travelled, term, arrived, behind, ahead, load,
     far_send, far_recv, near_send, near_recv, behind_send, behind_recv, ahead_send, ahead_recv,
+    gain_send, gain_recv, rows_send, rows_recv, innovation_send, innovation_recv,
 ):
     row = lax.axis_index("row")
     column = lax.axis_index("col")
@@ -62,12 +65,25 @@
     after = lax.rem(column + 1, column_total)
     mesh_id = pl.DeviceIdType.MESH
 
+    loads = [
+        pltpu.make_async_copy(source, target, load.at[at])
+        for at, (source, target) in enumerate(
+            ((covariance_in, covariance), (courants_in, courants), (noise_in, noise),
+             (targets_in, targets), (variance_in, variance))
+        )
+    ]
+    for transfer in loads:
+        transfer.start()
     barrier = pltpu.get_barrier_semaphore()
-    for peer in (far_target, far_source, partner):
+    for step in range(1, column_total):
+        peer = lax.rem(column + step, column_total)
+        pl.semaphore_signal(barrier, 1, device_id={"col": peer}, device_id_type=mesh_id)
+    for step in range(1, row_total):
+        peer = lax.rem(row + step, row_total)
         pl.semaphore_signal(barrier, 1, device_id={"row": peer}, device_id_type=mesh_id)
-    for peer in (before, after):
-        pl.semaphore_signal(barrier, 1, device_id={"col": peer}, device_id_type=mesh_id)
-    pl.semaphore_wait(barrier, 5)
+    for transfer in loads:
+        transfer.wait()
+    pl.semaphore_wait(barrier, row_total + column_total - 2)
 
     def chunk(k):
         return covariance.at[:, k * NC : (k + 1) * NC]
@@ -84,6 +100,10 @@
     ]
     for transfer in far:
         transfer.start()
+
+    stations = targets.shape[1]
+    row_share, column_share = stations // row_total, stations // column_total
+    sites[...] = jnp.broadcast_to(targets[...], (NC, stations)).T
 
     window = 2 * band_rows + 2 * CYCLES
     pair_first = (row - half) * band_rows - CYCLES + grid_rows
@@ -177,56 +197,16 @@
 
         lax.fori_loop(0, NC // step, piece, 0)
 
-    for transfer in far + near + sides:
-        transfer.wait_send()
-
-
-def forecast_call(covariance, courants, noise, row_total, column_total):
-    height, width = covariance.shape
-    band_rows, band_columns = height // NC, width // NC
-    vmem = pl.BlockSpec(memory_space=pltpu.VMEM)
-    lines = pltpu.VMEM((band_columns, height, NC), jnp.float32)
-    side = pltpu.VMEM((CYCLES, height, NC), jnp.float32)
-    window = 2 * band_rows + 2 * CYCLES
-    return pl.pallas_call(
-        functools.partial(forecast_kernel, row_total, column_total),
-        out_shape=jax.ShapeDtypeStruct(covariance.shape, jnp.float32),
-        in_specs=[vmem] * 3,
-        out_specs=vmem,
-        scratch_shapes=[pltpu.VMEM((CYCLES, 2, window, NC, NC), jnp.float32)]
-        + [lines] * 4
-        + [side] * 2
-        + [pltpu.SemaphoreType.DMA((band_columns,))] * 4
-        + [pltpu.SemaphoreType.DMA((CYCLES,))] * 4,
-        compiler_params=pltpu.CompilerParams(
-            collective_id=1, has_side_effects=True, vmem_limit_bytes=24 * 2**20
-        ),
-    )(covariance, courants, noise)
-
-
-def gather_kernel(
-    row_total, column_total, spread, row_sites, column_sites, gain, rows, innovation,
-    gain_all, rows_all, innovation_all,
-    gain_send, gain_recv, rows_send, rows_recv, innovation_send, innovation_recv,
-):
-    row = lax.axis_index("row")
-    column = lax.axis_index("col")
-    row_share, column_share = row_sites.shape[0], column_sites.shape[0]
-    barrier = pltpu.get_barrier_semaphore()
-    for step in range(1, column_total):
-        peer = lax.rem(column + step, column_total)
-        pl.semaphore_signal(barrier, 1, device_id={"col": peer}, device_id_type=pl.DeviceIdType.MESH)
-    for step in range(1, row_total):
-        peer = lax.rem(row + step, row_total)
-        pl.semaphore_signal(barrier, 1, device_id={"row": peer}, device_id_type=pl.DeviceIdType.MESH)
-
-    height, width = spread.shape
-    pick_rows = jnp.where(
-        row_sites[...] == lax.broadcasted_iota(jnp.int32, (row_share, height), 1), 1.0, 0.0
-    )
-    pick_columns = jnp.where(
-        column_sites[...] == lax.broadcasted_iota(jnp.int32, (column_share, width), 1), 1.0, 0.0
-    )
+    def picks(share, index, extent):
+        first = pl.multiple_of(index * share, share)
+        local = sites[pl.ds(first, share), :] - index * extent
+        lanes = lax.broadcasted_iota(jnp.int32, (share, NC), 1)
+        return jnp.concatenate(
+            [jnp.where(local == lanes + at, 1.0, 0.0) for at in range(0, extent, NC)], axis=1
+        )
+
+    pick_rows = picks(row_share, row, height)
+    pick_columns = picks(column_share, column, width)
 
     def gain_block(index):
         return gain_all.at[pl.ds(pl.multiple_of(index * column_share, column_share), column_share)]
@@ -238,25 +218,24 @@
         return innovation_all.at[pl.ds(pl.multiple_of(index * row_share, row_share), row_share)]
 
     gain_block(column)[...] = lax.dot_general(
-        pick_columns, spread[...], (((1,), (1,)), ((), ())),
+        pick_columns, out[...], (((1,), (1,)), ((), ())),
         precision=finest_accuracy, preferred_element_type=jnp.float32,
     )
     rows_block(row)[...] = jnp.dot(
-        pick_rows, spread[...], precision=finest_accuracy, preferred_element_type=jnp.float32
-    )
-    pl.semaphore_wait(barrier, row_total + column_total - 2)
+        pick_rows, out[...], precision=finest_accuracy, preferred_element_type=jnp.float32
+    )
 
     def exchange(block, me, axis, total, send, recv):
         copies = []
         for step in range(1, total):
             peer = lax.rem(me + step, total)
-            copy = pltpu.make_async_remote_copy(
+            transfer = pltpu.make_async_remote_copy(
                 src_ref=block(me), dst_ref=block(me),
                 send_sem=send.at[step], recv_sem=recv.at[step],
                 device_id={axis: peer}, device_id_type=pl.DeviceIdType.MESH,
             )
-            copy.start()
-            copies.append(copy)
+            transfer.start()
+            copies.append(transfer)
         return copies
 
     def arrive(block, me, axis, total, send, recv):
@@ -276,32 +255,56 @@
         precision=finest_accuracy, preferred_element_type=jnp.float32,
     )
     sent += exchange(innovation_block, row, "row", row_total, innovation_send, innovation_recv)
-    gain[...] = gain_all[...]
+    gain_out[...] = gain_all[...]
     arrive(rows_block, row, "row", row_total, rows_send, rows_recv)
-    rows[...] = rows_all[...]
+    rows_out[...] = rows_all[...]
     arrive(innovation_block, row, "row", row_total, innovation_send, innovation_recv)
-    innovation[...] = innovation_all[...]
-    for copy in sent:
-        copy.wait_send()
-
-
-def gather_call(spread, row_sites, column_sites, row_total, column_total):
-    height, width = spread.shape
-    stations = row_sites.shape[0] * row_total
+    square = (stations, stations)
+    diagonal = lax.broadcasted_iota(jnp.int32, square, 0) == lax.broadcasted_iota(
+        jnp.int32, square, 1
+    )
+    innovation_out[...] = innovation_all[...] + jnp.where(diagonal, variance[...], 0.0)
+    for transfer in far + near + sides + sent:
+        transfer.wait_send()
+
+
+def forecast_call(covariance, courants, noise, targets, variance, row_total, column_total):
+    height, width = covariance.shape
+    stations = targets.shape[0]
+    band_rows, band_columns = height // NC, width // NC
+    vmem = pl.BlockSpec(memory_space=pltpu.VMEM)
+    lines = pltpu.VMEM((band_columns, height, NC), jnp.float32)
+    side = pltpu.VMEM((CYCLES, height, NC), jnp.float32)
+    window = 2 * band_rows + 2 * CYCLES
     shapes = [(stations, height), (stations, width), (stations, stations)]
-    vmem = pl.BlockSpec(memory_space=pltpu.VMEM)
-    semaphores = [pltpu.SemaphoreType.DMA((column_total,))] * 2
-    semaphores += [pltpu.SemaphoreType.DMA((row_total,))] * 4
     return pl.pallas_call(
-        functools.partial(gather_kernel, row_total, column_total),
-        out_shape=[jax.ShapeDtypeStruct(shape, jnp.float32) for shape in shapes],
-        in_specs=[vmem] * 3,
-        out_specs=[vmem] * 3,
-        scratch_shapes=[pltpu.VMEM(shape, jnp.float32) for shape in shapes] + semaphores,
+        functools.partial(forecast_kernel, row_total, column_total),
+        out_shape=[
+            jax.ShapeDtypeStruct(shape, jnp.float32) for shape in [covariance.shape] + shapes
+        ],
+        in_specs=[pl.BlockSpec(memory_space=pltpu.HBM)] * 5,
+        out_specs=[vmem] * 4,
+        scratch_shapes=[
+            pltpu.VMEM(covariance.shape, jnp.float32),
+            pltpu.VMEM(courants.shape, jnp.float32),
+            pltpu.VMEM(noise.shape, jnp.float32),
+            pltpu.VMEM((1, stations), jnp.int32),
+            pltpu.VMEM((1, stations), jnp.float32),
+            pltpu.VMEM((stations, NC), jnp.int32),
+        ]
+        + [pltpu.VMEM(shape, jnp.float32) for shape in shapes]
+        + [pltpu.VMEM((CYCLES, 2, window, NC, NC), jnp.float32)]
+        + [lines] * 4
+        + [side] * 2
+        + [pltpu.SemaphoreType.DMA((5,))]
+        + [pltpu.SemaphoreType.DMA((band_columns,))] * 4
+        + [pltpu.SemaphoreType.DMA((CYCLES,))] * 4
+        + [pltpu.SemaphoreType.DMA((column_total,))] * 2
+        + [pltpu.SemaphoreType.DMA((row_total,))] * 4,
         compiler_params=pltpu.CompilerParams(
-            collective_id=0, has_side_effects=True, vmem_limit_bytes=24 * 2**20
+            collective_id=0, has_side_effects=True, vmem_limit_bytes=40 * 2**20
         ),
-    )(spread, row_sites[:, None], column_sites[:, None])
+    )(covariance, courants, noise, targets[None, :], variance[None, :])
 
 
 PIVOTS = 4
@@ -374,13 +377,9 @@
     return jnp.concatenate(parts, axis=0)
 
 
-def analysis_kernel(spread, innovation, noise, rows, gain, out):
-    stations = innovation.shape[0]
-    diagonal = lax.broadcasted_iota(jnp.int32, (stations, stations), 0) == lax.broadcasted_iota(
-        jnp.int32, (stations, stations), 1
-    )
+def analysis_kernel(spread, innovation, rows, gain, out):
     matrix = innovation[...]
-    matrix = (matrix + matrix.T) * 0.5 + jnp.where(diagonal, noise[...], 0.0)
+    matrix = (matrix + matrix.T) * 0.5
     inverse = invert(matrix)
     weighted = jnp.dot(
         inverse, rows[...], precision=finest_accuracy, preferred_element_type=jnp.float32
@@ -391,10 +390,10 @@
     )
 
 
-def analysis_call(spread, innovation, noise, rows, gain):
+def analysis_call(spread, innovation, rows, gain):
     stations = innovation.shape[0]
     if stations > NC:
-        factor = jnp.linalg.cholesky(innovation + jnp.diag(noise))
+        factor = jnp.linalg.cholesky(innovation)
         inverse = jax.scipy.linalg.solve_triangular(
             factor, jnp.eye(stations, dtype=jnp.float32), lower=True
         )
@@ -407,36 +406,18 @@
     return pl.pallas_call(
         analysis_kernel,
         out_shape=jax.ShapeDtypeStruct(spread.shape, jnp.float32),
-        in_specs=[vmem] * 5,
+        in_specs=[vmem] * 4,
         out_specs=vmem,
         compiler_params=pltpu.CompilerParams(vmem_limit_bytes=24 * 2**20),
-    )(spread, innovation, noise[None, :], rows, gain)
+    )(spread, innovation, rows, gain)
 
 
 def per_device(covariance, courants, process_noise_spread, sensor_targets, noise_variance):
-    row_index = lax.axis_index("row")
-    column_index = lax.axis_index("col")
-    row_total = lax.axis_size("row")
-    column_total = lax.axis_size("col")
-    horizontal_tile_piece, vertical_tile_piece = covariance.shape
-    predicted_spread = forecast_call(
-        covariance, courants, process_noise_spread, row_total, column_total
-    )
-    station_total = sensor_targets.shape[0]
-    row_share = station_total // row_total
-    column_share = station_total // column_total
-    sensor_horizontal_indices = (
-        lax.dynamic_slice_in_dim(sensor_targets, row_index * row_share, row_share)
-        - row_index * horizontal_tile_piece
-    )
-    sensor_vertical_indices = (
-        lax.dynamic_slice_in_dim(sensor_targets, column_index * column_share, column_share)
-        - column_index * vertical_tile_piece
-    )
-    gain, rows, innovation = gather_call(
-        predicted_spread, sensor_horizontal_indices, sensor_vertical_indices, row_total, column_total
-    )
-    return analysis_call(predicted_spread, innovation, noise_variance, rows, gain)
+    spread, gain, rows, innovation = forecast_call(
+        covariance, courants, process_noise_spread, sensor_targets, noise_variance,
+        lax.axis_size("row"), lax.axis_size("col"),
+    )
+    return analysis_call(spread, innovation, rows, gain)
 
 
 def solution(mesh):

time: 51.8 us -> 48.6 us (0.938)
  Pallas kernels: 47.6 us -> 45.9 us
  other arithmetic: 1.46 us -> 0 us
    pallas_call x1 -> x0, Pallas kernels: 11.3 us -> none  [gather_call(): pl.pallas_call(functools.partial(gather_kernel, row_total, column_total),...]
    pallas_call x1, Pallas kernels: 28.2 us -> 37.7 us  [forecast_call(): pl.pallas_call(functools.partial(forecast_kernel, row_total, column_total...]
    broadcast_in_dim x2 -> x0, other arithmetic: 1.46 us -> none  [the longest x1 0.74 us: gather_call(): column_sites[:, None]]
    unnamed x8 -> x10, local copies, waits for them, and re-layouts: 2.28 us -> 2.49 us
where the time goes in v3:
time: 48.6 us; the launch traced here: 48.4 us
  Pallas kernels  45.9 us (94%)
  local copies, waits for them, and re-layouts  2.49 us (5%)
    pallas_call x1, Pallas kernels, forecast_call(): pl.pallas_call(functools.partial(forecast_kernel, row_total, column_total...  37.7 us
    pallas_call x1, Pallas kernels, analysis_call(): pl.pallas_call(analysis_kernel, out_shape=jax.ShapeDtypeStruct(spread.sha...  8.14 us
    unnamed x10, local copies, waits for them, and re-layouts  2.49 us

profile of v3, /device:TPU:0, one launch (start us, length us, event | category | flops | bytes accessed | tf_op | source)
XLA Modules:
  0.0 48.4 jit_solution(16062172683159590393)
XLA Ops:
  0.0 0.0 copy-start.4
  0.0 0.0 copy-start.2
  0.0 0.0 copy-start.3
  0.0 0.6 %copy-done.4 = f32[128]{0:T(128)S(1)} copy-done((f32[128]{0:T(128)S(1)}, f32[128]{0:T(128)}, u32[]{:S(2)}) %copy-start.4) | copy-done | bytes 536
  0.7 0.0 copy-done.2
  0.7 0.0 copy-done.3
  0.7 0.0 copy-start
  0.7 1.0 %copy-done = f32[256,512]{1,0:T(8,128)S(1)} copy-done((f32[256,512]{1,0:T(8,128)S(1)}, f32[256,512]{1,0:T(8,128)}, u32[]{:S(2)}) %copy-start) | copy-done | bytes 524312
  1.7 0.0 copy-start.1
  1.7 0.8 %copy-done.1 = f32[2,2,16,128]{3,2,1,0:T(8,128)S(1)} copy-done((f32[2,2,16,128]{3,2,1,0:T(8,128)S(1)}, f32[2,2,16,128]{3,2,1,0:T(8,128)}, u32[]{:S(2)}) %copy-start.1) | copy-done | bytes 32792
  2.5 37.7 %shard_map.55 = (f32[256,512]{1,0:T(8,128)S(1)}, f32[128,256]{1,0:T(8,128)S(1)}, f32[128,512]{1,0:T(8,128)S(1)}, f32[128,128]{1,0:T(8,128)S(1)}) custom-call(f32[256,512]{1,0:T(8,128)S(1)} %copy-done, f32[2,2,16,128]{3,2,1,0:T(8,128)S(1)} %copy-done.1, f32[2,128]{1,0:T(2,128)S(1)} %copy-done.2, s32[1,128]{1,0:T(1,128)S(1)} %bitcast.2, f32[1,128]{1,0:T(1,128)S(1)} %bitcast.3), custom_call_target="tpu_custom_call" | custom-call | tf_op jit(solution)/shard_map/pallas_call | solution.py:280
  40.2 8.1 %shard_map.56 = f32[256,512]{1,0:T(8,128)} custom-call(f32[256,512]{1,0:T(8,128)S(1)} %get-tuple-element.9.spread, f32[128,128]{1,0:T(8,128)S(1)} %get-tuple-element.10.innovation, f32[128,512]{1,0:T(8,128)S(1)} %get-tuple-element.11.rows, f32[128,256]{1,0:T(8,128)S(1)} %get-tuple-element.12.gain), custom_call_target="tpu_custom_call" | custom-call | tf_op jit(solution)/shard_map/pallas_call | solution.py:406
Async XLA Ops:
  0.0 0.7 %copy-start.4 = (f32[128]{0:T(128)S(1)}, f32[128]{0:T(128)}, u32[]{:S(2)}) copy-start(f32[128]{0:T(128)} %param.9) | copy-start | bytes 1540
  0.0 0.7 %copy-start.2 = (f32[2,128]{1,0:T(2,128)S(1)}, f32[2,128]{1,0:T(2,128)}, u32[]{:S(2)}) copy-start(f32[2,128]{1,0:T(2,128)} %noise_in.1) | copy-start | bytes 3076
  0.0 0.7 %copy-start.3 = (s32[128]{0:T(128)S(1)}, s32[128]{0:T(128)}, u32[]{:S(2)}) copy-start(s32[128]{0:T(128)} %param.8) | copy-start | bytes 1540
  0.7 1.0 %copy-start = (f32[256,512]{1,0:T(8,128)S(1)}, f32[256,512]{1,0:T(8,128)}, u32[]{:S(2)}) copy-start(f32[256,512]{1,0:T(8,128)} %covariance_in.1) | copy-start | bytes 1572868
  1.7 0.8 %copy-start.1 = (f32[2,2,16,128]{3,2,1,0:T(8,128)S(1)}, f32[2,2,16,128]{3,2,1,0:T(8,128)}, u32[]{:S(2)}) copy-start(f32[2,2,16,128]{3,2,1,0:T(8,128)} %courants_in.1) | copy-start | bytes 98308

commit v4 on v3

--- a/solution.py
+++ b/solution.py
@@ -42,6 +42,19 @@
             for at in range(1, len(stack) - 1)
         ]
     return stack
+
+
+def select(pick, values, contract):
+    pick = pick.astype(jnp.bfloat16)
+    total = None
+    for _ in range(3):
+        part = values.astype(jnp.bfloat16)
+        values = values - part.astype(jnp.float32)
+        product = lax.dot_general(
+            pick, part, (contract, ((), ())), preferred_element_type=jnp.float32
+        )
+        total = product if total is None else total + product
+    return total
 
 
 def forecast_kernel(
@@ -131,22 +144,35 @@
 
     lax.fori_loop(0, band_columns, own_part, 0)
 
+    def line_of(buffer, k, i):
+        return buffer.at[k, i * NC : (i + 1) * NC]
+
     near = [
-        copy(term.at[k], arrived.at[k], near_send, near_recv, k, "row", partner)
+        [
+            copy(line_of(term, k, i), line_of(arrived, k, i), near_send, near_recv,
+                 k * band_rows + i, "row", partner)
+            for i in range(band_rows)
+        ]
         for k in range(band_columns)
     ]
-    sides = []
+    sides = [[] for _ in range(band_rows)]
 
     def finish(k):
-        near[k].wait_recv()
-        done[k] = done[k] + arrived[k]
-        if k < CYCLES:
-            sides.append(copy(done.at[k], ahead.at[k], ahead_send, ahead_recv, k, "col", before))
-            sides[-1].start()
-        if k >= band_columns - CYCLES:
-            at = k - (band_columns - CYCLES)
-            sides.append(copy(done.at[k], behind.at[at], behind_send, behind_recv, at, "col", after))
-            sides[-1].start()
+        for i in range(band_rows):
+            near[k][i].wait_recv()
+            rows = slice(i * NC, (i + 1) * NC)
+            done[k, rows, :] = done[k, rows, :] + arrived[k, rows, :]
+            if k < CYCLES:
+                transfer = copy(line_of(done, k, i), line_of(ahead, k, i), ahead_send, ahead_recv,
+                                k * band_rows + i, "col", before)
+                transfer.start()
+                sides[i].append(transfer)
+            if k >= band_columns - CYCLES:
+                at = k - (band_columns - CYCLES)
+                transfer = copy(line_of(done, k, i), line_of(behind, at, i), behind_send,
+                                behind_recv, at * band_rows + i, "col", after)
+                transfer.start()
+                sides[i].append(transfer)
 
     for k in range(band_columns):
         far[k].wait_recv()
@@ -159,12 +185,10 @@
         lines = advance(lower + [None] * band_rows + upper, winds_of(other_offset), 0)
         for i, line in enumerate(lines):
             term[k, i * NC : (i + 1) * NC, :] = line
-        near[k].start()
+            near[k][i].start()
         if k:
             finish(k - 1)
     finish(band_columns - 1)
-    for transfer in sides:
-        transfer.wait_recv()
 
     column_first = column * band_columns - CYCLES + grid_rows
     column_winds = {
@@ -177,6 +201,8 @@
     }
     step = 32
     for i in range(band_rows):
+        for transfer in sides[i]:
+            transfer.wait_recv()
         cell_noise = noise[i : i + 1, :]
 
         def piece(m, _):
@@ -217,13 +243,7 @@
     def innovation_block(index):
         return innovation_all.at[pl.ds(pl.multiple_of(index * row_share, row_share), row_share)]
 
-    gain_block(column)[...] = lax.dot_general(
-        pick_columns, out[...], (((1,), (1,)), ((), ())),
-        precision=finest_accuracy, preferred_element_type=jnp.float32,
-    )
-    rows_block(row)[...] = jnp.dot(
-        pick_rows, out[...], precision=finest_accuracy, preferred_element_type=jnp.float32
-    )
+    gain_block(column)[...] = select(pick_columns, out[...], ((1,), (1,)))
 
     def exchange(block, me, axis, total, send, recv):
         copies = []
@@ -248,12 +268,10 @@
             ).wait_recv()
 
     sent = exchange(gain_block, column, "col", column_total, gain_send, gain_recv)
+    rows_block(row)[...] = select(pick_rows, out[...], ((1,), (0,)))
     sent += exchange(rows_block, row, "row", row_total, rows_send, rows_recv)
     arrive(gain_block, column, "col", column_total, gain_send, gain_recv)
-    innovation_block(row)[...] = lax.dot_general(
-        pick_rows, gain_all[...], (((1,), (1,)), ((), ())),
-        precision=finest_accuracy, preferred_element_type=jnp.float32,
-    )
+    innovation_block(row)[...] = select(pick_rows, gain_all[...], ((1,), (1,)))
     sent += exchange(innovation_block, row, "row", row_total, innovation_send, innovation_recv)
     gain_out[...] = gain_all[...]
     arrive(rows_block, row, "row", row_total, rows_send, rows_recv)
@@ -264,7 +282,7 @@
         jnp.int32, square, 1
     )
     innovation_out[...] = innovation_all[...] + jnp.where(diagonal, variance[...], 0.0)
-    for transfer in far + near + sides + sent:
+    for transfer in far + sum(near + sides, []) + sent:
         transfer.wait_send()
 
 
@@ -297,8 +315,9 @@
         + [lines] * 4
         + [side] * 2
         + [pltpu.SemaphoreType.DMA((5,))]
-        + [pltpu.SemaphoreType.DMA((band_columns,))] * 4
-        + [pltpu.SemaphoreType.DMA((CYCLES,))] * 4
+        + [pltpu.SemaphoreType.DMA((band_columns,))] * 2
+        + [pltpu.SemaphoreType.DMA((band_columns * band_rows,))] * 2
+        + [pltpu.SemaphoreType.DMA((CYCLES * band_rows,))] * 4
         + [pltpu.SemaphoreType.DMA((column_total,))] * 2
         + [pltpu.SemaphoreType.DMA((row_total,))] * 4,
         compiler_params=pltpu.CompilerParams(

time: 48.6 us -> 48 us (0.988)
  Pallas kernels: 45.9 us -> 45.3 us
    pallas_call x1, Pallas kernels: 37.7 us -> 37.1 us  [forecast_call(): pl.pallas_call(functools.partial(forecast_kernel, row_total, column_total...]
where the time goes in v4:
time: 48 us; the launch traced here: 47.8 us
  Pallas kernels  45.3 us (94%)
  local copies, waits for them, and re-layouts  2.49 us (5%)
    pallas_call x1, Pallas kernels, forecast_call(): pl.pallas_call(functools.partial(forecast_kernel, row_total, column_total...  37.1 us
    pallas_call x1, Pallas kernels, analysis_call(): pl.pallas_call(analysis_kernel, out_shape=jax.ShapeDtypeStruct(spread.sha...  8.14 us
    unnamed x10, local copies, waits for them, and re-layouts  2.49 us

profile of v4, /device:TPU:0, one launch (start us, length us, event | category | flops | bytes accessed | tf_op | source)
XLA Modules:
  0.0 47.8 jit_solution(2516679919075860159)
XLA Ops:
  0.0 0.0 copy-start.4
  0.0 0.0 copy-start.2
  0.0 0.0 copy-start.3
  0.0 0.6 %copy-done.4 = f32[128]{0:T(128)S(1)} copy-done((f32[128]{0:T(128)S(1)}, f32[128]{0:T(128)}, u32[]{:S(2)}) %copy-start.4) | copy-done | bytes 536
  0.7 0.0 copy-done.2
  0.7 0.0 copy-done.3
  0.7 0.0 copy-start
  0.7 1.0 %copy-done = f32[256,512]{1,0:T(8,128)S(1)} copy-done((f32[256,512]{1,0:T(8,128)S(1)}, f32[256,512]{1,0:T(8,128)}, u32[]{:S(2)}) %copy-start) | copy-done | bytes 524312
  1.7 0.0 copy-start.1
  1.7 0.8 %copy-done.1 = f32[2,2,16,128]{3,2,1,0:T(8,128)S(1)} copy-done((f32[2,2,16,128]{3,2,1,0:T(8,128)S(1)}, f32[2,2,16,128]{3,2,1,0:T(8,128)}, u32[]{:S(2)}) %copy-start.1) | copy-done | bytes 32792
  2.5 37.1 %shard_map.55 = (f32[256,512]{1,0:T(8,128)S(1)}, f32[128,256]{1,0:T(8,128)S(1)}, f32[128,512]{1,0:T(8,128)S(1)}, f32[128,128]{1,0:T(8,128)S(1)}) custom-call(f32[256,512]{1,0:T(8,128)S(1)} %copy-done, f32[2,2,16,128]{3,2,1,0:T(8,128)S(1)} %copy-done.1, f32[2,128]{1,0:T(2,128)S(1)} %copy-done.2, s32[1,128]{1,0:T(1,128)S(1)} %bitcast.2, f32[1,128]{1,0:T(1,128)S(1)} %bitcast.3), custom_call_target="tpu_custom_call" | custom-call | tf_op jit(solution)/shard_map/pallas_call | solution.py:298
  39.6 8.1 %shard_map.56 = f32[256,512]{1,0:T(8,128)} custom-call(f32[256,512]{1,0:T(8,128)S(1)} %get-tuple-element.9.spread, f32[128,128]{1,0:T(8,128)S(1)} %get-tuple-element.10.innovation, f32[128,512]{1,0:T(8,128)S(1)} %get-tuple-element.11.rows, f32[128,256]{1,0:T(8,128)S(1)} %get-tuple-element.12.gain), custom_call_target="tpu_custom_call" | custom-call | tf_op jit(solution)/shard_map/pallas_call | solution.py:425
Async XLA Ops:
  0.0 0.7 %copy-start.4 = (f32[128]{0:T(128)S(1)}, f32[128]{0:T(128)}, u32[]{:S(2)}) copy-start(f32[128]{0:T(128)} %param.9) | copy-start | bytes 1540
  0.0 0.7 %copy-start.2 = (f32[2,128]{1,0:T(2,128)S(1)}, f32[2,128]{1,0:T(2,128)}, u32[]{:S(2)}) copy-start(f32[2,128]{1,0:T(2,128)} %noise_in.1) | copy-start | bytes 3076
  0.0 0.7 %copy-start.3 = (s32[128]{0:T(128)S(1)}, s32[128]{0:T(128)}, u32[]{:S(2)}) copy-start(s32[128]{0:T(128)} %param.8) | copy-start | bytes 1540
  0.7 1.0 %copy-start = (f32[256,512]{1,0:T(8,128)S(1)}, f32[256,512]{1,0:T(8,128)}, u32[]{:S(2)}) copy-start(f32[256,512]{1,0:T(8,128)} %covariance_in.1) | copy-start | bytes 1572868
  1.7 0.8 %copy-start.1 = (f32[2,2,16,128]{3,2,1,0:T(8,128)S(1)}, f32[2,2,16,128]{3,2,1,0:T(8,128)}, u32[]{:S(2)}) copy-start(f32[2,2,16,128]{3,2,1,0:T(8,128)} %courants_in.1) | copy-start | bytes 98308

commit v5 on v4

--- a/solution.py
+++ b/solution.py
@@ -321,7 +321,7 @@
         + [pltpu.SemaphoreType.DMA((column_total,))] * 2
         + [pltpu.SemaphoreType.DMA((row_total,))] * 4,
         compiler_params=pltpu.CompilerParams(
-            collective_id=0, has_side_effects=True, vmem_limit_bytes=40 * 2**20
+            collective_id=0, has_side_effects=True, vmem_limit_bytes=61 * 2**20
         ),
     )(covariance, courants, noise, targets[None, :], variance[None, :])
 
@@ -396,10 +396,23 @@
     return jnp.concatenate(parts, axis=0)
 
 
-def analysis_kernel(spread, innovation, rows, gain, out):
+def analysis_kernel(
+    spread_in, innovation_in, rows_in, gain_in, out, spread, innovation, rows, gain, load
+):
+    loads = [
+        pltpu.make_async_copy(source, target, load.at[at])
+        for at, (source, target) in enumerate(
+            ((innovation_in, innovation), (rows_in, rows), (gain_in, gain), (spread_in, spread))
+        )
+    ]
+    for transfer in loads:
+        transfer.start()
+    loads[0].wait()
     matrix = innovation[...]
     matrix = (matrix + matrix.T) * 0.5
     inverse = invert(matrix)
+    for transfer in loads[1:]:
+        transfer.wait()
     weighted = jnp.dot(
         inverse, rows[...], precision=finest_accuracy, preferred_element_type=jnp.float32
     )
@@ -425,9 +438,13 @@
     return pl.pallas_call(
         analysis_kernel,
         out_shape=jax.ShapeDtypeStruct(spread.shape, jnp.float32),
-        in_specs=[vmem] * 4,
+        in_specs=[pl.BlockSpec(memory_space=pltpu.HBM)] * 4,
         out_specs=vmem,
-        compiler_params=pltpu.CompilerParams(vmem_limit_bytes=24 * 2**20),
+        scratch_shapes=[
+            pltpu.VMEM(array.shape, jnp.float32) for array in (spread, innovation, rows, gain)
+        ]
+        + [pltpu.SemaphoreType.DMA((4,))],
+        compiler_params=pltpu.CompilerParams(vmem_limit_bytes=61 * 2**20),
     )(spread, innovation, rows, gain)
 
 

time: 48 us -> 47.2 us (0.983)
  local copies, waits for them, and re-layouts: 2.49 us -> 0 us
  Pallas kernels: 45.3 us -> 47.1 us
    unnamed x10 -> x0, local copies, waits for them, and re-layouts: 2.49 us -> none
    pallas_call x1, Pallas kernels: 8.14 us -> 9.08 us  [analysis_call(): pl.pallas_call(analysis_kernel, out_shape=jax.ShapeDtypeStruct(spread.sha...]
    pallas_call x1, Pallas kernels: 37.1 us -> 38 us  [forecast_call(): pl.pallas_call(functools.partial(forecast_kernel, row_total, column_total...]
where the time goes in v5:
time: 47.2 us; the launch traced here: 47.1 us
  Pallas kernels  47.1 us (100%)
    pallas_call x1, Pallas kernels, forecast_call(): pl.pallas_call(functools.partial(forecast_kernel, row_total, column_total...  38 us
    pallas_call x1, Pallas kernels, analysis_call(): pl.pallas_call(analysis_kernel, out_shape=jax.ShapeDtypeStruct(spread.sha...  9.08 us

profile of v5, /device:TPU:0, one launch (start us, length us, event | category | flops | bytes accessed | tf_op | source)
XLA Modules:
  0.0 47.1 jit_solution(11545607093637928793)
XLA Ops:
  0.0 38.0 %shard_map.55 = (f32[256,512]{1,0:T(8,128)}, f32[128,256]{1,0:T(8,128)}, f32[128,512]{1,0:T(8,128)}, f32[128,128]{1,0:T(8,128)}) custom-call(f32[256,512]{1,0:T(8,128)} %covariance_in.1, f32[2,2,16,128]{3,2,1,0:T(8,128)} %courants_in.1, f32[2,128]{1,0:T(2,128)} %noise_in.1, s32[1,128]{1,0:T(1,128)} %bitcast.2, f32[1,128]{1,0:T(1,128)} %bitcast.3), custom_call_target="tpu_custom_call" | custom-call | tf_op jit(solution)/shard_map/pallas_call | solution.py:298
  38.0 9.1 %shard_map.56 = f32[256,512]{1,0:T(8,128)} custom-call(f32[256,512]{1,0:T(8,128)} %get-tuple-element.9.spread_in, f32[128,128]{1,0:T(8,128)} %get-tuple-element.10.innovation_in, f32[128,512]{1,0:T(8,128)} %get-tuple-element.11.rows_in, f32[128,256]{1,0:T(8,128)} %get-tuple-element.12.gain_in), custom_call_target="tpu_custom_call" | custom-call | tf_op jit(solution)/shard_map/pallas_call | solution.py:438

commit v6 on v5

--- a/solution.py
+++ b/solution.py
@@ -59,8 +59,8 @@
 
 def forecast_kernel(
     row_total, column_total, covariance_in, courants_in, noise_in, targets_in, variance_in,
-    out, gain_out, rows_out, innovation_out,
-    covariance, courants, noise, targets, variance, sites, gain_all, rows_all, innovation_all,
+    spread_out, gain_out, rows_out, innovation_out,
+    out, summed, store, covariance, courants, noise, targets, variance, sites, gain_all, rows_all, innovation_all,
     wind, done, travelled, term, arrived, behind, ahead, load,
     far_send, far_recv, near_send, near_recv, behind_send, behind_recv, ahead_send, ahead_recv,
     gain_send, gain_recv, rows_send, rows_recv, innovation_send, innovation_recv,
@@ -231,6 +231,12 @@
             [jnp.where(local == lanes + at, 1.0, 0.0) for at in range(0, extent, NC)], axis=1
         )
 
+    def keep(source, target, at):
+        stores.append(pltpu.make_async_copy(source, target, store.at[at]))
+        stores[-1].start()
+
+    stores = []
+    keep(out, spread_out, 0)
     pick_rows = picks(row_share, row, height)
     pick_columns = picks(column_share, column, width)
 
@@ -273,15 +279,18 @@
     arrive(gain_block, column, "col", column_total, gain_send, gain_recv)
     innovation_block(row)[...] = select(pick_rows, gain_all[...], ((1,), (1,)))
     sent += exchange(innovation_block, row, "row", row_total, innovation_send, innovation_recv)
-    gain_out[...] = gain_all[...]
+    keep(gain_all, gain_out, 1)
     arrive(rows_block, row, "row", row_total, rows_send, rows_recv)
-    rows_out[...] = rows_all[...]
+    keep(rows_all, rows_out, 2)
     arrive(innovation_block, row, "row", row_total, innovation_send, innovation_recv)
     square = (stations, stations)
     diagonal = lax.broadcasted_iota(jnp.int32, square, 0) == lax.broadcasted_iota(
         jnp.int32, square, 1
     )
-    innovation_out[...] = innovation_all[...] + jnp.where(diagonal, variance[...], 0.0)
+    summed[...] = innovation_all[...] + jnp.where(diagonal, variance[...], 0.0)
+    keep(summed, innovation_out, 3)
+    for transfer in stores:
+        transfer.wait()
     for transfer in far + sum(near + sides, []) + sent:
         transfer.wait_send()
 
@@ -290,7 +299,6 @@
     height, width = covariance.shape
     stations = targets.shape[0]
     band_rows, band_columns = height // NC, width // NC
-    vmem = pl.BlockSpec(memory_space=pltpu.VMEM)
     lines = pltpu.VMEM((band_columns, height, NC), jnp.float32)
     side = pltpu.VMEM((CYCLES, height, NC), jnp.float32)
     window = 2 * band_rows + 2 * CYCLES
@@ -301,8 +309,11 @@
             jax.ShapeDtypeStruct(shape, jnp.float32) for shape in [covariance.shape] + shapes
         ],
         in_specs=[pl.BlockSpec(memory_space=pltpu.HBM)] * 5,
-        out_specs=[vmem] * 4,
+        out_specs=[pl.BlockSpec(memory_space=pltpu.HBM)] * 4,
         scratch_shapes=[
+            pltpu.VMEM(covariance.shape, jnp.float32),
+            pltpu.VMEM((stations, stations), jnp.float32),
+            pltpu.SemaphoreType.DMA((4,)),
             pltpu.VMEM(covariance.shape, jnp.float32),
             pltpu.VMEM(courants.shape, jnp.float32),
             pltpu.VMEM(noise.shape, jnp.float32),

time: 47.2 us -> 46.9 us (level)
  no operation moved by 1% of the time
where the time goes in v6:
time: 46.9 us; the launch traced here: 46.8 us
  Pallas kernels  46.8 us (100%)
    pallas_call x1, Pallas kernels, forecast_call(): pl.pallas_call(functools.partial(forecast_kernel, row_total, column_total...  37.7 us
    pallas_call x1, Pallas kernels, analysis_call(): pl.pallas_call(analysis_kernel, out_shape=jax.ShapeDtypeStruct(spread.sha...  9.07 us

profile of v6, /device:TPU:0, one launch (start us, length us, event | category | flops | bytes accessed | tf_op | source)
XLA Modules:
  0.0 46.8 jit_solution(14370395524478382704)
XLA Ops:
  0.0 37.7 %shard_map.55 = (f32[256,512]{1,0:T(8,128)}, f32[128,256]{1,0:T(8,128)}, f32[128,512]{1,0:T(8,128)}, f32[128,128]{1,0:T(8,128)}) custom-call(f32[256,512]{1,0:T(8,128)} %covariance_in.1, f32[2,2,16,128]{3,2,1,0:T(8,128)} %courants_in.1, f32[2,128]{1,0:T(2,128)} %noise_in.1, s32[1,128]{1,0:T(1,128)} %bitcast.2, f32[1,128]{1,0:T(1,128)} %bitcast.3), custom_call_target="tpu_custom_call" | custom-call | tf_op jit(solution)/shard_map/pallas_call | solution.py:306
  37.7 9.1 %shard_map.56 = f32[256,512]{1,0:T(8,128)} custom-call(f32[256,512]{1,0:T(8,128)} %get-tuple-element.9.spread_in, f32[128,128]{1,0:T(8,128)} %get-tuple-element.10.innovation_in, f32[128,512]{1,0:T(8,128)} %get-tuple-element.11.rows_in, f32[128,256]{1,0:T(8,128)} %get-tuple-element.12.gain_in), custom_call_target="tpu_custom_call" | custom-call | tf_op jit(solution)/shard_map/pallas_call | solution.py:449
